TPU v7x, 32 devices: a whole 2x2x4 slice. The times are simulated.
32 devices in a mesh: rep: 8 (over y, x, core), shard: 4 (over z).
Axes of the slice: x: 2, y: 2, z: 4, core: 2. Of those that a mesh axis runs over, the one named last changes fastest.
Arguments:
- tokens: bfloat16 [32768, 1024], P(('rep', 'shard')), may hold values from -6 to 6
- segments: int32 [32, 1024], P(('rep', 'shard')), may hold values from 0 to 3, never falling along the last dimension, each value on 1 to 768 neighbouring positions
- ln1_gain: bfloat16 [1024], P('shard'), may hold values from 0.099609375 to 1.8984375
- ln1_bias: bfloat16 [1024], P('shard'), may hold values from -3 to 3
- w_qkv: bfloat16 [1024, 3072], P('shard'), may hold values from -0.1875 to 0.1875
- q_bias: bfloat16 [1024], P('shard'), may hold values from -3 to 3
- v_bias: bfloat16 [1024], P('shard'), may hold values from -3 to 3
- w_out: bfloat16 [1024, 1024], P('shard'), may hold values from -0.5 to 0.5
- out_bias: bfloat16 [1024], P('shard'), may hold values from -3 to 3
- ln2_gain: bfloat16 [1024], P('shard'), may hold values from 0.099609375 to 1.8984375
- ln2_bias: bfloat16 [1024], P('shard'), may hold values from -3 to 3
- w_up: bfloat16 [1024, 4096], P('shard'), may hold values from -0.1875 to 0.1875
- up_bias: bfloat16 [4096], P('shard'), may hold values from -3 to 3
- w_down: bfloat16 [4096, 1024], P('shard'), may hold values from -0.09375 to 0.09375
- down_bias: bfloat16 [1024], P('shard'), may hold values from -3 to 3
- cotangent: bfloat16 [32768, 1024], P(('rep', 'shard')), may hold values from -6 to 6
Outputs:
- output: bfloat16 [32768, 1024], P(('rep', 'shard'))
- token_grad: bfloat16 [32768, 1024], P(('rep', 'shard'))
- ln1_gain_grad: float32 [1024], P('shard')
- ln1_bias_grad: float32 [1024], P('shard')
- w_qkv_grad: float32 [1024, 3072], P('shard')
- q_bias_grad: float32 [1024], P('shard')
- v_bias_grad: float32 [1024], P('shard')
- w_out_grad: float32 [1024, 1024], P('shard')
- out_bias_grad: float32 [1024], P('shard')
- ln2_gain_grad: float32 [1024], P('shard')
- ln2_bias_grad: float32 [1024], P('shard')
- w_up_grad: float32 [1024, 4096], P('shard')
- up_bias_grad: float32 [4096], P('shard')
- w_down_grad: float32 [4096, 1024], P('shard')
- down_bias_grad: float32 [1024], P('shard')
Inputs may be any that keep to these rules, and one draw needn't show every extreme that they name: `segments`: within each sequence the numbers start at 0, never fall and name every document 0 to 3; each document has at most 768 tokens and one has exactly 768.
All inputs are finite; a program needn't handle non-finite values.
Results may differ from a plain program's by a relative error of at most 0.014.
Values may be sent and summed in bfloat16 or wider, within the bound.
A program may use at most 320 MiB of HBM per device.

v0:
```python
import jax
import jax.numpy as jnp
from jax import lax
from jax.sharding import PartitionSpec as P

HEADS = 16


EPS = 1e-05
GELU_C = 0.7978845608028654
GELU_A = 0.044715


def normalize(values):
    centred = values - jnp.mean(values, axis=-1, keepdims=True)
    scale = lax.rsqrt(jnp.mean(centred * centred, axis=-1, keepdims=True) + EPS)
    return (centred * scale, scale)


def norm_back(grad_h, normed, scale, gain):
    grad_n = grad_h * gain
    return scale * (
        grad_n
        - jnp.mean(grad_n, axis=-1, keepdims=True)
        - normed * jnp.mean(grad_n * normed, axis=-1, keepdims=True)
    )


def left_dot(left, right):
    return lax.dot_general(
        left, right, (((0,), (0,)), ((), ())), preferred_element_type=jnp.float32
    )


def right_dot(left, right):
    return lax.dot_general(
        left, right, (((1,), (1,)), ((), ())), preferred_element_type=jnp.float32
    )


def column_sum(values):
    return jnp.sum(values.astype(jnp.float32), axis=0)


def block_scores(q_blk, keys, s_blk, seg, slopes, start):
    block = q_blk.shape[0]
    rows = keys.shape[0]
    raw = jnp.einsum("qhd,khd->hqk", q_blk, keys, preferred_element_type=jnp.float32) * q_blk.shape[
        2
    ] ** (-0.5)
    query_pos = start + jnp.arange(block, dtype=jnp.int32)
    key_pos = jnp.arange(rows, dtype=jnp.int32)
    dist = (key_pos[None, :] - query_pos[:, None]).astype(jnp.float32)
    scores = raw + slopes[:, None, None] * dist[None]
    allowed = (key_pos[None, :] <= query_pos[:, None]) & (s_blk[:, None] == seg[None, :])
    return jnp.where(allowed[None], scores, -1e30)


def shards(
    tokens,
    segments,
    ln1_gain,
    ln1_bias,
    w_qkv,
    q_bias,
    v_bias,
    w_out,
    out_bias,
    ln2_gain,
    ln2_bias,
    w_up,
    up_bias,
    w_down,
    down_bias,
    cotangent,
):
    gathered = (
        lax.all_gather(ln1_gain, "shard", axis=0, tiled=True),
        lax.all_gather(ln1_bias, "shard", axis=0, tiled=True),
        lax.all_gather(w_qkv, "shard", axis=0, tiled=True),
        lax.all_gather(q_bias, "shard", axis=0, tiled=True),
        lax.all_gather(v_bias, "shard", axis=0, tiled=True),
        lax.all_gather(w_out, "shard", axis=0, tiled=True),
        lax.all_gather(out_bias, "shard", axis=0, tiled=True),
        lax.all_gather(ln2_gain, "shard", axis=0, tiled=True),
        lax.all_gather(ln2_bias, "shard", axis=0, tiled=True),
        lax.all_gather(w_up, "shard", axis=0, tiled=True),
        lax.all_gather(up_bias, "shard", axis=0, tiled=True),
        lax.all_gather(w_down, "shard", axis=0, tiled=True),
        lax.all_gather(down_bias, "shard", axis=0, tiled=True),
    )
    (
        first_gain,
        first_shift,
        qkv_matrix,
        query_bias,
        value_bias,
        out_matrix,
        out_shift,
        second_gain,
        second_shift,
        up_matrix,
        up_shift,
        down_matrix,
        down_shift,
    ) = gathered
    rows, width = tokens.shape
    heads = HEADS
    head_dim = width // heads
    block = min(512, rows)
    count = rows // block
    seg = segments[0]
    slopes = 2.0 ** (-8.0 * (jnp.arange(heads, dtype=jnp.float32) + 1.0) / heads)
    scale = head_dim ** (-0.5)
    inputs = tokens.astype(jnp.float32)
    normed_one, scale_one = normalize(inputs)
    first = (normed_one * first_gain.astype(jnp.float32) + first_shift.astype(jnp.float32)).astype(
        jnp.bfloat16
    )
    joined = jnp.concatenate([query_bias, jnp.zeros_like(query_bias), value_bias]).astype(
        jnp.float32
    )
    qkv = (jnp.dot(first, qkv_matrix, preferred_element_type=jnp.float32) + joined).astype(
        jnp.bfloat16
    )
    query = qkv[:, :width].reshape(rows, heads, head_dim)
    keys = qkv[:, width : 2 * width].reshape(rows, heads, head_dim)
    values = qkv[:, 2 * width :].reshape(rows, heads, head_dim)
    query_blocks = query.reshape(count, block, heads, head_dim)
    seg_blocks = seg.reshape(count, block)
    starts = jnp.arange(count, dtype=jnp.int32) * block

    def forward_block(item):
        q_blk, s_blk, start = item
        scores = block_scores(q_blk, keys, s_blk, seg, slopes, start)
        top = jnp.max(scores, axis=-1, keepdims=True)
        weights = jnp.exp(scores - top)
        total = jnp.sum(weights, axis=-1, keepdims=True)
        probs = (weights / total).astype(jnp.bfloat16)
        mixed_blk = jnp.einsum("hqk,khd->qhd", probs, values, preferred_element_type=jnp.float32)
        return (mixed_blk.astype(jnp.bfloat16), (top + jnp.log(total))[:, :, 0])

    mixed_blocks, lse_blocks = lax.map(forward_block, (query_blocks, seg_blocks, starts))
    mixed = mixed_blocks.reshape(rows, width)
    middle = (
        inputs
        + jnp.dot(mixed, out_matrix, preferred_element_type=jnp.float32)
        + out_shift.astype(jnp.float32)
    )
    normed_two, scale_two = normalize(middle)
    second = (
        normed_two * second_gain.astype(jnp.float32) + second_shift.astype(jnp.float32)
    ).astype(jnp.bfloat16)
    upper = jnp.dot(second, up_matrix, preferred_element_type=jnp.float32) + up_shift.astype(
        jnp.float32
    )
    tanh_value = jnp.tanh(GELU_C * (upper + GELU_A * upper * upper * upper))
    active = (0.5 * upper * (1.0 + tanh_value)).astype(jnp.bfloat16)
    output = (
        middle
        + jnp.dot(active, down_matrix, preferred_element_type=jnp.float32)
        + down_shift.astype(jnp.float32)
    ).astype(jnp.bfloat16)
    first_gain, qkv_matrix, out_matrix, second_gain, up_matrix, down_matrix = (
        lax.all_gather(ln1_gain, "shard", axis=0, tiled=True),
        lax.all_gather(w_qkv, "shard", axis=0, tiled=True),
        lax.all_gather(w_out, "shard", axis=0, tiled=True),
        lax.all_gather(ln2_gain, "shard", axis=0, tiled=True),
        lax.all_gather(w_up, "shard", axis=0, tiled=True),
        lax.all_gather(w_down, "shard", axis=0, tiled=True),
    )
    down_shift_grad = column_sum(cotangent)
    down_grad = left_dot(active, cotangent)
    grad_active = right_dot(cotangent, down_matrix)
    gelu_slope = 0.5 * (1.0 + tanh_value) + 0.5 * upper * (
        1.0 - tanh_value * tanh_value
    ) * GELU_C * (1.0 + 3.0 * GELU_A * upper * upper)
    grad_upper = (grad_active * gelu_slope).astype(jnp.bfloat16)
    up_shift_grad = column_sum(grad_upper)
    up_grad = left_dot(second, grad_upper)
    grad_second = right_dot(grad_upper, up_matrix)
    second_gain_grad = jnp.sum(grad_second * normed_two, axis=0)
    second_shift_grad = jnp.sum(grad_second, axis=0)
    grad_middle = cotangent.astype(jnp.float32) + norm_back(
        grad_second, normed_two, scale_two, second_gain.astype(jnp.float32)
    )
    grad_branch = grad_middle.astype(jnp.bfloat16)
    out_shift_grad = column_sum(grad_branch)
    out_grad = left_dot(mixed, grad_branch)
    grad_mixed = right_dot(grad_branch, out_matrix).astype(jnp.bfloat16)
    grad_mixed_blocks = grad_mixed.reshape(count, block, heads, head_dim)

    def backward_block(carry, item):
        grad_keys, grad_values = carry
        q_blk, gm_blk, s_blk, start, lse_blk = item
        scores = block_scores(q_blk, keys, s_blk, seg, slopes, start)
        probs = jnp.exp(scores - lse_blk[:, :, None])
        grad_probs = jnp.einsum("qhd,khd->hqk", gm_blk, values, preferred_element_type=jnp.float32)
        inner = jnp.sum(probs * grad_probs, axis=-1, keepdims=True)
        grad_scores = (probs * (grad_probs - inner)).astype(jnp.bfloat16)
        grad_query = (
            jnp.einsum("hqk,khd->qhd", grad_scores, keys, preferred_element_type=jnp.float32)
            * scale
        )
        grad_keys = (
            grad_keys
            + jnp.einsum("hqk,qhd->khd", grad_scores, q_blk, preferred_element_type=jnp.float32)
            * scale
        )
        grad_values = grad_values + jnp.einsum(
            "hqk,qhd->khd", probs.astype(jnp.bfloat16), gm_blk, preferred_element_type=jnp.float32
        )
        return ((grad_keys, grad_values), grad_query.astype(jnp.bfloat16))

    empty = jnp.zeros((rows, heads, head_dim), jnp.float32)
    (grad_keys, grad_values), grad_query_blocks = lax.scan(
        backward_block,
        (empty, empty),
        (query_blocks, grad_mixed_blocks, seg_blocks, starts, lse_blocks),
    )
    grad_qkv = jnp.concatenate(
        [
            grad_query_blocks.reshape(rows, width),
            grad_keys.reshape(rows, width).astype(jnp.bfloat16),
            grad_values.reshape(rows, width).astype(jnp.bfloat16),
        ],
        axis=1,
    )
    query_bias_grad = column_sum(grad_qkv[:, :width])
    value_bias_grad = column_sum(grad_qkv[:, 2 * width :])
    qkv_grad = left_dot(first, grad_qkv)
    grad_first = right_dot(grad_qkv, qkv_matrix)
    first_gain_grad = jnp.sum(grad_first * normed_one, axis=0)
    first_shift_grad = jnp.sum(grad_first, axis=0)
    token_grad = (
        grad_middle + norm_back(grad_first, normed_one, scale_one, first_gain.astype(jnp.float32))
    ).astype(jnp.bfloat16)
    shares = (
        lax.psum_scatter(
            first_gain_grad.astype(jnp.bfloat16), "shard", scatter_dimension=0, tiled=True
        ).astype(jnp.float32),
        lax.psum_scatter(
            first_shift_grad.astype(jnp.bfloat16), "shard", scatter_dimension=0, tiled=True
        ).astype(jnp.float32),
        lax.psum_scatter(
            qkv_grad.astype(jnp.bfloat16), "shard", scatter_dimension=0, tiled=True
        ).astype(jnp.float32),
        lax.psum_scatter(
            query_bias_grad.astype(jnp.bfloat16), "shard", scatter_dimension=0, tiled=True
        ).astype(jnp.float32),
        lax.psum_scatter(
            value_bias_grad.astype(jnp.bfloat16), "shard", scatter_dimension=0, tiled=True
        ).astype(jnp.float32),
        lax.psum_scatter(
            out_grad.astype(jnp.bfloat16), "shard", scatter_dimension=0, tiled=True
        ).astype(jnp.float32),
        lax.psum_scatter(
            out_shift_grad.astype(jnp.bfloat16), "shard", scatter_dimension=0, tiled=True
        ).astype(jnp.float32),
        lax.psum_scatter(
            second_gain_grad.astype(jnp.bfloat16), "shard", scatter_dimension=0, tiled=True
        ).astype(jnp.float32),
        lax.psum_scatter(
            second_shift_grad.astype(jnp.bfloat16), "shard", scatter_dimension=0, tiled=True
        ).astype(jnp.float32),
        lax.psum_scatter(
            up_grad.astype(jnp.bfloat16), "shard", scatter_dimension=0, tiled=True
        ).astype(jnp.float32),
        lax.psum_scatter(
            up_shift_grad.astype(jnp.bfloat16), "shard", scatter_dimension=0, tiled=True
        ).astype(jnp.float32),
        lax.psum_scatter(
            down_grad.astype(jnp.bfloat16), "shard", scatter_dimension=0, tiled=True
        ).astype(jnp.float32),
        lax.psum_scatter(
            down_shift_grad.astype(jnp.bfloat16), "shard", scatter_dimension=0, tiled=True
        ).astype(jnp.float32),
    )
    summed = lax.psum(
        (
            shares[0],
            shares[1],
            shares[2],
            shares[3],
            shares[4],
            shares[5],
            shares[6],
            shares[7],
            shares[8],
            shares[9],
            shares[10],
            shares[11],
            shares[12],
        ),
        "rep",
    )
    return (
        output,
        token_grad,
        summed[0],
        summed[1],
        summed[2],
        summed[3],
        summed[4],
        summed[5],
        summed[6],
        summed[7],
        summed[8],
        summed[9],
        summed[10],
        summed[11],
        summed[12],
    )


def solution(mesh):
    in_specs = (
        P(("rep", "shard"), None),
        P(("rep", "shard"), None),
        P("shard"),
        P("shard"),
        P("shard", None),
        P("shard"),
        P("shard"),
        P("shard", None),
        P("shard"),
        P("shard"),
        P("shard"),
        P("shard", None),
        P("shard"),
        P("shard", None),
        P("shard"),
        P(("rep", "shard"), None),
    )
    out_specs = (
        P(("rep", "shard"), None),
        P(("rep", "shard"), None),
        P("shard"),
        P("shard"),
        P("shard", None),
        P("shard"),
        P("shard"),
        P("shard", None),
        P("shard"),
        P("shard"),
        P("shard"),
        P("shard", None),
        P("shard"),
        P("shard", None),
        P("shard"),
    )
    return jax.shard_map(shards, mesh=mesh, in_specs=in_specs, out_specs=out_specs, check_vma=False)
```

profile of v0, /device:TPU:0, one launch (start us, length us, event | category | flops | bytes accessed | tf_op | source)
XLA Modules:
  0.0 1452.7 jit_solution(3306852074069905306)
XLA Ops:
  10.3 12.6 all-gather.6
  80.9 15.8 %all_gather.55 = bf16[4096]{0:T(1024)(128)(2,1)S(1)} all-gather(bf16[1024]{0:T(1024)(128)(2,1)S(1)} %copy-done.39), channel_id=1, replica_groups=mesh['rep'=8,'shard'=4] {'shard'}, dimensions={0}, use_global_device_ids=true | all-gather | bytes 10240 | tf_op jit(solution)/shard_map/all_gather | solution.py:88
  105.2 23.1 %all-gather.13.cloned.1.call-done = bf16[1024,3072]{1,0:T(8,128)(2,1)} async-done(((bf16[256,3072]{1,0:T(8,128)(2,1)}), bf16[1024,3072]{1,0:T(8,128)(2,1)}) %all-gather.13.cloned.1.call-update) | async-done | bytes 6291472 | tf_op jit(solution)/shard_map/all_gather | solution.py:80
  159.0 105.9 %while.28 = (s32[]{:T(128)}, bf16[2,512,16,64]{1,3,2,0:T(8,128)(2,1)S(1)}, f32[2,16,512]{2,1,0:T(8,128)S(1)}, s32[2]{0:T(128)S(1)}, s32[2,512]{1,0:T(2,128)S(1)}...) while((s32[]{:T(128)}, ...), condition=%wide.region_5.6_spmd.clone, body=%wide.region_2.5_spmd.clone.sunk | while | flops 2301616640 | bytes 117719880 | solution.py:143
  161.2 17.1 %fusion.116 = (f32[16,512]{1,0:T(8,128)S(1)}, f32[16,512,1024]{2,1,0:T(8,128)}) fusion(f32[512,1024]{1,0:T(8,128)S(1)} %subtract_convert_fusion.4, f32[16]{0:T(128)S(1)} %multiply_power_fusion.4, pred[512,1024]{1,0:T(8,128)(4,1)S(1)} %fusion.115, bf16[1024,16,64]{0,2,1:T(8,128)(2,1)} %get-tuple-element.565, ...), kind=kOutput, calls=%fused_computation.6.clone.1 | convolution fusion | flops 1115676672 | bytes 39354436 | tf_op jit(solution)/shard_map/while/body/eval_jaxpr/qhd,khd->hqk/dot_general | solution.py:48
  178.4 17.1 %fusion.117 = f32[16,512]{1,0:T(8,128)S(1)} fusion(f32[16,512,1024]{2,1,0:T(8,128)} %get-tuple-element.522, f32[16,512]{1,0:T(8,128)S(1)} %get-tuple-element.523, f32[512,1024]{1,0:T(8,128)S(1)} %subtract_convert_fusion.4, f32[16]{0:T(128)S(1)} %multiply_power_fusion.4, pred[512,1024]{1,0:T(8,128)(4,1)S(1)} %fusion.115), kind=kLoop, calls=%fused_computation.5.clone.1 | loop fusion | flops 50323456 | bytes 36241472 | tf_op jit(solution)/shard_map/while/body/eval_jaxpr/reduce_sum | solution.py:138
  195.5 16.7 %fusion.118 = bf16[2,512,16,64]{1,3,2,0:T(8,128)(2,1)S(1)} fusion(bf16[2,512,16,64]{1,3,2,0:T(8,128)(2,1)S(1)} %get-tuple-element.549, s32[]{:T(128)S(6)} %copy.98, bf16[1024,16,64]{0,2,1:T(8,128)(2,1)} %get-tuple-element.566, f32[16,512,1024]{2,1,0:T(8,128)} %get-tuple-element.522, f32[16,512]{1,0:T(8,128)S(1)} %fusion.117, ...), kind=kOutput, calls=%fused_computation.13.clone.1 | convolution fusion | flops 1132986368 | bytes 39387652 | tf_op jit(solution)/shard_map/while/body/eval_jaxpr/hqk,khd->qhd/dot_general | solution.py:140
  214.2 17.2 %fusion.116 = (f32[16,512]{1,0:T(8,128)S(1)}, f32[16,512,1024]{2,1,0:T(8,128)}) fusion(f32[512,1024]{1,0:T(8,128)S(1)} %subtract_convert_fusion.4, f32[16]{0:T(128)S(1)} %multiply_power_fusion.4, pred[512,1024]{1,0:T(8,128)(4,1)S(1)} %fusion.115, bf16[1024,16,64]{0,2,1:T(8,128)(2,1)} %get-tuple-element.565, ...), kind=kOutput, calls=%fused_computation.6.clone.1 | convolution fusion | flops 1115676672 | bytes 39354436 | tf_op jit(solution)/shard_map/while/body/eval_jaxpr/qhd,khd->hqk/dot_general | solution.py:48
  231.4 16.3 %fusion.117 = f32[16,512]{1,0:T(8,128)S(1)} fusion(f32[16,512,1024]{2,1,0:T(8,128)} %get-tuple-element.522, f32[16,512]{1,0:T(8,128)S(1)} %get-tuple-element.523, f32[512,1024]{1,0:T(8,128)S(1)} %subtract_convert_fusion.4, f32[16]{0:T(128)S(1)} %multiply_power_fusion.4, pred[512,1024]{1,0:T(8,128)(4,1)S(1)} %fusion.115), kind=kLoop, calls=%fused_computation.5.clone.1 | loop fusion | flops 50323456 | bytes 36241472 | tf_op jit(solution)/shard_map/while/body/eval_jaxpr/reduce_sum | solution.py:138
  247.7 16.8 %fusion.118 = bf16[2,512,16,64]{1,3,2,0:T(8,128)(2,1)S(1)} fusion(bf16[2,512,16,64]{1,3,2,0:T(8,128)(2,1)S(1)} %get-tuple-element.549, s32[]{:T(128)S(6)} %copy.98, bf16[1024,16,64]{0,2,1:T(8,128)(2,1)} %get-tuple-element.566, f32[16,512,1024]{2,1,0:T(8,128)} %get-tuple-element.522, f32[16,512]{1,0:T(8,128)S(1)} %fusion.117, ...), kind=kOutput, calls=%fused_computation.13.clone.1 | convolution fusion | flops 1132986368 | bytes 39387652 | tf_op jit(solution)/shard_map/while/body/eval_jaxpr/hqk,khd->qhd/dot_general | solution.py:140
  279.7 44.1 %all-gather.17.cloned.1.call-done = bf16[1024,4096]{1,0:T(8,128)(2,1)} async-done(((bf16[256,4096]{1,0:T(8,128)(2,1)}), bf16[1024,4096]{1,0:T(8,128)(2,1)}) %all-gather.17.cloned.1.call-update) | async-done | bytes 8388624 | tf_op jit(solution)/shard_map/all_gather | solution.py:87
  323.8 17.0 %fusion.67 = f32[1024,4096]{1,0:T(8,128)} fusion(bf16[1024,4096]{1,0:T(8,128)(2,1)} %all-gather.17.cloned.1.call-done, f32[1024,1024]{0,1:T(8,128)} %copy-done.5, f32[1024]{0:T(1024)S(1)} %bitcast.163, f32[1024]{0:T(1024)S(1)} %bitcast.155, f32[1024]{0:T(1024)S(1)} %add_rsqrt_fusion, f32[1024]{0:T(1024)S(1)} %broadcast_multiply_fusion.4), kind=kOutput, calls=%fused_computation.124 | convolution fusion | flops 8595177472 | bytes 29376512 | tf_op jit(solution)/shard_map/dot_general | solution.py:154
  340.8 132.3 %all-gather.19.cloned.1.call-done = bf16[4096,1024]{1,0:T(8,128)(2,1)} async-done(((bf16[1024,1024]{1,0:T(8,128)(2,1)}), bf16[4096,1024]{1,0:T(8,128)(2,1)}) %all-gather.19.cloned.1.call-update) | async-done | bytes 8388624 | tf_op jit(solution)/shard_map/all_gather | solution.py:89
  473.1 23.9 %fusion.73 = (bf16[4096]{0:T(1024)(128)(2,1)}, bf16[1024,4096]{1,0:T(8,128)(2,1)}) fusion(f32[1024,4096]{1,0:T(8,128)} %fusion.67, f32[4096]{0:T(1024)S(1)} %copy-done.29, bf16[1024,1024]{1,0:T(8,128)(2,1)S(1)} %copy-done.12, bf16[4096,1024]{1,0:T(8,128)(2,1)} %all-gather.19.cloned.1.call-done), kind=kOutput, calls=%fused_computation.130 | convolution fusion | flops 8678010880 | bytes 35676160 | tf_op jit(solution)/shard_map/dot_general | solution.py:36
  497.0 15.6 %fusion.72 = (bf16[1024]{0:T(1024)(128)(2,1)}, f32[1024,1024]{1,0:T(8,128)}) fusion(bf16[1024,4096]{1,0:T(8,128)(2,1)} %get-tuple-element.399, bf16[1024,4096]{1,0:T(8,128)(2,1)} %all-gather.17.cloned.1.call-done), kind=kOutput, calls=%fused_computation.129 | convolution fusion | flops 8590982144 | bytes 20973568 | tf_op jit(solution)/shard_map/dot_general | solution.py:36
  548.9 220.8 %while.29 = (s32[]{:T(128)}, f32[1024,16,64]{0,2,1:T(8,128)}, f32[1024,16,64]{0,2,1:T(8,128)}, bf16[2,512,16,64]{1,3,2,0:T(8,128)(2,1)}, bf16[2,512,16,64]{1,3,2...) while((s32[]{:T(128)}, f32[1024,16,64]{0,2,1:T(8,128)}, ...), condition=%wide.region_12.13_spmd.clone, body=%wide.region_10.12_spmd.clone.sunk | while | flops 5469889024 | bytes 352502080 | solution.py:216
  551.3 17.7 %fusion.128 = f32[16,512,1024]{2,1,0:T(8,128)} fusion(bf16[1024,16,64]{0,2,1:T(8,128)(2,1)} %get-tuple-element.607, bf16[2,512,16,64]{1,3,2,0:T(8,128)(2,1)} %get-tuple-element.606, s32[]{:T(128)S(6)} %copy.108), kind=kOutput, calls=%fused_computation.38.clone.1 | convolution fusion | flops 1073741824 | bytes 36700164 | tf_op jit(solution)/shard_map/while/body/eval_jaxpr/qhd,khd->hqk/dot_general | solution.py:198
  569.0 27.9 %multiply_reduce_fusion.7 = (f32[16,512]{1,0:T(8,128)S(1)}, f32[16,512,1024]{2,1,0:T(8,128)}) fusion(f32[16,512,1024]{2,1,0:T(8,128)} %fusion.128, f32[16,512]{1,0:T(8,128)S(1)} %dynamic-slice_bitcast_fusion.2, f32[512,1024]{1,0:T(8,128)S(1)} %subtract_convert_fusion.5, f32[16]{0:T(128)S(1)} %multiply_power_fusion.5, ...), kind=kOutput, calls=%fused_computation.25.clone.1 | convolution fusion | flops 1132453888 | bytes 72941632 | tf_op jit(solution)/shard_map/while/body/eval_jaxpr/qhd,khd->hqk/dot_general | solution.py:48
  596.9 27.4 %multiply_convert_fusion.6 = bf16[16,512,1024]{2,1,0:T(8,128)(2,1)} fusion(f32[16,512,1024]{2,1,0:T(8,128)} %get-tuple-element.536, f32[16,512,1024]{2,1,0:T(8,128)} %fusion.128, f32[16,512]{1,0:T(8,128)S(1)} %get-tuple-element.537), kind=kLoop, calls=%fused_computation.24.clone.1 | loop fusion | flops 25165824 | bytes 83918848 | tf_op jit(solution)/shard_map/while/body/eval_jaxpr/convert_element_type | solution.py:200
  624.3 16.0 %bitcast_add_fusion.5 = f32[1024,16,64]{0,2,1:T(8,128)} fusion(f32[1024,16,64]{0,2,1:T(8,128)} %get-tuple-element.584, f32[16,512,1024]{2,1,0:T(8,128)} %get-tuple-element.536, pred[]{:T(512)S(6)} %compare.3, bf16[2,512,16,64]{1,3,2,0:T(8,128)(2,1)} %get-tuple-element.606, s32[]{:T(128)S(6)} %copy.108), kind=kOutput, calls=%fused_computation.29.clone.1 | convolution fusion | flops 1084227584 | bytes 42991620 | tf_op jit(solution)/shard_map/while/body/eval_jaxpr/hqk,qhd->khd/dot_general | solution.py:210
  660.3 17.5 %fusion.128 = f32[16,512,1024]{2,1,0:T(8,128)} fusion(bf16[1024,16,64]{0,2,1:T(8,128)(2,1)} %get-tuple-element.607, bf16[2,512,16,64]{1,3,2,0:T(8,128)(2,1)} %get-tuple-element.606, s32[]{:T(128)S(6)} %copy.108), kind=kOutput, calls=%fused_computation.38.clone.1 | convolution fusion | flops 1073741824 | bytes 36700164 | tf_op jit(solution)/shard_map/while/body/eval_jaxpr/qhd,khd->hqk/dot_general | solution.py:198
  677.8 27.9 %multiply_reduce_fusion.7 = (f32[16,512]{1,0:T(8,128)S(1)}, f32[16,512,1024]{2,1,0:T(8,128)}) fusion(f32[16,512,1024]{2,1,0:T(8,128)} %fusion.128, f32[16,512]{1,0:T(8,128)S(1)} %dynamic-slice_bitcast_fusion.2, f32[512,1024]{1,0:T(8,128)S(1)} %subtract_convert_fusion.5, f32[16]{0:T(128)S(1)} %multiply_power_fusion.5, ...), kind=kOutput, calls=%fused_computation.25.clone.1 | convolution fusion | flops 1132453888 | bytes 72941632 | tf_op jit(solution)/shard_map/while/body/eval_jaxpr/qhd,khd->hqk/dot_general | solution.py:48
  705.7 27.4 %multiply_convert_fusion.6 = bf16[16,512,1024]{2,1,0:T(8,128)(2,1)} fusion(f32[16,512,1024]{2,1,0:T(8,128)} %get-tuple-element.536, f32[16,512,1024]{2,1,0:T(8,128)} %fusion.128, f32[16,512]{1,0:T(8,128)S(1)} %get-tuple-element.537), kind=kLoop, calls=%fused_computation.24.clone.1 | loop fusion | flops 25165824 | bytes 83918848 | tf_op jit(solution)/shard_map/while/body/eval_jaxpr/convert_element_type | solution.py:200
  733.1 17.1 %bitcast_add_fusion.5 = f32[1024,16,64]{0,2,1:T(8,128)} fusion(f32[1024,16,64]{0,2,1:T(8,128)} %get-tuple-element.584, f32[16,512,1024]{2,1,0:T(8,128)} %get-tuple-element.536, pred[]{:T(512)S(6)} %compare.3, bf16[2,512,16,64]{1,3,2,0:T(8,128)(2,1)} %get-tuple-element.606, s32[]{:T(128)S(6)} %copy.108), kind=kOutput, calls=%fused_computation.29.clone.1 | convolution fusion | flops 1084227584 | bytes 42991620 | tf_op jit(solution)/shard_map/while/body/eval_jaxpr/hqk,qhd->khd/dot_general | solution.py:210
  791.4 19.6 %convolution_convert_fusion = bf16[4096,1024]{1,0:T(8,128)(2,1)} fusion(bf16[1024,1024]{1,0:T(8,128)(2,1)} %param.35, f32[1024,4096]{1,0:T(8,128)} %fusion.67, f32[4096]{0:T(1024)S(1)} %copy-done.30), kind=kOutput, calls=%fused_computation.65 | convolution fusion | flops 8636071936 | bytes 27279360 | tf_op jit(solution)/shard_map/dot_general | solution.py:30
  811.7 15.4 %convolution_convert_fusion.1 = bf16[1024,4096]{1,0:T(8,128)(2,1)} fusion(bf16[1024,4096]{1,0:T(8,128)(2,1)} %get-tuple-element.399, f32[1024,1024]{0,1:T(8,128)} %copy-done.5, f32[1024]{0:T(1024)S(1)} %bitcast.164, f32[1024]{0:T(1024)S(1)} %bitcast.158, f32[1024]{0:T(1024)S(1)} %copy-done.28, f32[1024]{0:T(1024)S(1)} %copy-done.20), kind=kOutput, calls=%fused_computation.66 | convolution fusion | flops 8599371776 | bytes 20987904 | tf_op jit(solution)/shard_map/dot_general | solution.py:30
  839.7 17.1 %add_convert_fusion.1 = bf16[1024,1024]{0,1:T(8,128)(2,1)} fusion(f32[1024,1024]{0,1:T(8,128)} %copy-done.5, f32[1024]{0:T(1024)S(1)} %bitcast.168, bf16[4096,1024]{1,0:T(8,128)(2,1)} %all-gather.19.cloned.1.call-done, f32[1024,4096]{1,0:T(8,128)} %fusion.67, f32[4096]{0:T(1024)S(1)} %copy-done.30), kind=kOutput, calls=%fused_computation.91 | convolution fusion | flops 8635023360 | bytes 31477760 | tf_op jit(solution)/shard_map/dot_general | solution.py:161
  862.9 12.1 fusion.71
  893.1 20.4 %all-reduce.10 = (bf16[1024]{0:T(1024)(128)(2,1)S(1)}, bf16[1024]{0:T(1024)(128)(2,1)S(1)}, bf16[1024]{0:T(1024)(128)(2,1)S(1)}, bf16[1024]{0:T(1024)(128)(2,1)S...) all-reduce(bf16[1024]{0:T(1024)(128)(2,1)S(1)} %get-tuple-element.3, ...), channel_id=2, replica_groups=mesh['rep'=8,'shard'=4] {'shard'}, use_global_device_ids=true, to_apply=%region_16.17.clone | all-reduce | flops 12288 | bytes 49152
  914.1 133.5 %reduce-scatter.11.cloned.1.call-done = bf16[1024,1024]{1,0:T(8,128)(2,1)} async-done(((bf16[4096,1024]{1,0:T(8,128)(2,1)}), bf16[1024,1024]{1,0:T(8,128)(2,1)}) %reduce-scatter.11.cloned.1.call-update) | async-done | bytes 2097168 | tf_op jit(solution)/shard_map/reduce_scatter | solution.py:272
  1047.5 147.8 %reduce-scatter.9.cloned.1.call-done = bf16[256,4096]{1,0:T(8,128)(2,1)} async-done(((bf16[1024,4096]{1,0:T(8,128)(2,1)}), bf16[256,4096]{1,0:T(8,128)(2,1)}) %reduce-scatter.9.cloned.1.call-update) | async-done | bytes 2097168 | tf_op jit(solution)/shard_map/reduce_scatter | solution.py:266
  1195.3 250.1 %all-reduce.12 = (f32[256]{0:T(256)}, f32[256]{0:T(256)}, f32[256,3072]{1,0:T(8,128)}, f32[256]{0:T(256)}, f32[256]{0:T(256)}, /*index=5*/f32[256,1024]{1,0:T(8,...) all-reduce(f32[256]{0:T(256)S(1)} %dynamic-slice_convert_fusion.8, ...), channel_id=1, replica_groups=mesh['rep'=8,'shard'=4] {'rep'}, use_global_device_ids=true, to_apply=%region_17.18 | all-reduce | flops 3148800 | bytes 18898944 | tf_op jit(solution)/shard_map/psum | solution.py:279
  (242 shorter events, 254.3 us)
Async XLA Ops:
  7.3 73.0 %copy-start.16 = (s32[1,1024]{1,0:T(1,128)S(1)}, s32[1,1024]{1,0:T(1,128)}, u32[]{:S(2)}) copy-start(s32[1,1024]{1,0:T(1,128)} %param.21) | copy-start | bytes 12292
  7.3 73.6 %copy-start.39 = (bf16[1024]{0:T(1024)(128)(2,1)S(1)}, bf16[1024]{0:T(1024)(128)(2,1)}, u32[]{:S(2)}) copy-start(bf16[1024]{0:T(1024)(128)(2,1)} %param.32) | copy-start | bytes 6148
  7.3 121.0 %all-gather.13.cloned.1.call-start = ((), (), s32[]{:S(2)}) async-start(), calls=%async_computation.4 | async-start | bytes 7864320 | tf_op jit(solution)/shard_map/all_gather | solution.py:80
  8.0 264.1 %all-gather.15.cloned.1.call-start = ((), (), s32[]{:S(2)}) async-start(), calls=%async_computation.5 | async-start | bytes 2621440 | tf_op jit(solution)/shard_map/all_gather | solution.py:83
  8.8 315.0 %all-gather.17.cloned.1.call-start = ((), (), s32[]{:S(2)}) async-start(), calls=%async_computation.6 | async-start | bytes 10485760 | tf_op jit(solution)/shard_map/all_gather | solution.py:87
  9.5 463.6 %all-gather.19.cloned.1.call-start = ((), (), s32[]{:S(2)}) async-start(), calls=%async_computation.7 | async-start | bytes 10485760 | tf_op jit(solution)/shard_map/all_gather | solution.py:89
  10.1 904.0 %reduce-scatter.7.cloned.1.call-start = ((), (), s32[]{:S(2)}) async-start(), calls=%async_computation.9 | async-start | bytes 2621440 | tf_op jit(solution)/shard_map/reduce_scatter | solution.py:254
  71.1 57.1 %copy-start.36 = (f32[4,1,256]{2,1,0:T(1,128)}, f32[4,1,256]{2,1,0:T(1,128)S(1)}, u32[]{:S(2)}) copy-start(f32[4,1,256]{2,1,0:T(1,128)S(1)} %convert_element_type.229) | copy-start | bytes 12292
  79.7 48.5 %copy-start.21 = (f32[4,1,256]{2,1,0:T(1,128)}, f32[4,1,256]{2,1,0:T(1,128)S(1)}, u32[]{:S(2)}) copy-start(f32[4,1,256]{2,1,0:T(1,128)S(1)} %convert_element_type.228) | copy-start | bytes 12292
  100.2 28.0 %copy-start.2 = (bf16[1024,1024]{0,1:T(8,128)(2,1)}, bf16[1024,1024]{0,1:T(8,128)(2,1)S(1)}, u32[]{:S(2)}) copy-start(bf16[1024,1024]{0,1:T(8,128)(2,1)S(1)} %copy.65) | copy-start | bytes 6291460
  100.6 38.0 %copy-start.17 = (f32[1024]{0:T(1024)}, f32[1024]{0:T(1024)S(1)}, u32[]{:S(2)}) copy-start(f32[1024]{0:T(1024)S(1)} %broadcast_multiply_fusion.5) | copy-start | bytes 12292
  101.2 37.4 %copy-start.23 = (f32[1024]{0:T(1024)}, f32[1024]{0:T(1024)S(1)}, u32[]{:S(2)}) copy-start(f32[1024]{0:T(1024)S(1)} %add_rsqrt_fusion.1) | copy-start | bytes 12292
  266.3 5.8 copy-start.3
  266.3 5.8 copy-start.38
  277.2 46.6 %copy-start.25 = (f32[4,1,256]{2,1,0:T(1,128)S(1)}, f32[4,1,256]{2,1,0:T(1,128)}, u32[]{:S(2)}) copy-start(f32[4,1,256]{2,1,0:T(1,128)} %convert_element_type.231) | copy-start | bytes 12292
  277.2 46.6 %copy-start.34 = (f32[4,1,256]{2,1,0:T(1,128)S(1)}, f32[4,1,256]{2,1,0:T(1,128)}, u32[]{:S(2)}) copy-start(f32[4,1,256]{2,1,0:T(1,128)} %convert_element_type.232) | copy-start | bytes 12292
  277.2 246.1 %copy-start.19 = (f32[1024]{0:T(1024)}, f32[1024]{0:T(1024)S(1)}, u32[]{:S(2)}) copy-start(f32[1024]{0:T(1024)S(1)} %broadcast_multiply_fusion.4) | copy-start | bytes 12292
  279.7 243.6 %copy-start.27 = (f32[1024]{0:T(1024)}, f32[1024]{0:T(1024)S(1)}, u32[]{:S(2)}) copy-start(f32[1024]{0:T(1024)S(1)} %add_rsqrt_fusion) | copy-start | bytes 12292
  323.8 149.3 %copy-start.12 = (bf16[1024,1024]{1,0:T(8,128)(2,1)S(1)}, bf16[1024,1024]{1,0:T(8,128)(2,1)}, u32[]{:S(2)}) copy-start(bf16[1024,1024]{1,0:T(8,128)(2,1)} %param.35) | copy-start | bytes 6291460
  323.8 149.3 %copy-start.29 = (f32[4096]{0:T(1024)S(1)}, f32[4096]{0:T(1024)}, u32[]{:S(2)}) copy-start(f32[4096]{0:T(1024)} %convert_element_type.194) | copy-start | bytes 49156
  512.6 10.7 copy-start.11
  518.1 5.2 copy-start.6
  518.1 5.9 copy-start.7
  524.1 4.8 copy-start.15
  532.6 381.5 %reduce-scatter.5.cloned.1.call-start = ((), (), s32[]{:S(2)}) async-start(), calls=%async_computation.8 | async-start | bytes 7864320 | tf_op jit(solution)/shard_map/reduce_scatter | solution.py:245
  640.3 11.5 copy-start
  750.2 11.5 copy-start
  772.3 5.9 copy-start.14
  772.5 4.1 copy-start.1
  790.7 256.8 %reduce-scatter.11.cloned.1.call-start = ((), (), s32[]{:S(2)}) async-start(), calls=%async_computation.11 | async-start | bytes 10485760 | tf_op jit(solution)/shard_map/reduce_scatter | solution.py:272
  811.1 384.2 %reduce-scatter.9.cloned.1.call-start = ((), (), s32[]{:S(2)}) async-start(), calls=%async_computation.10 | async-start | bytes 10485760 | tf_op jit(solution)/shard_map/reduce_scatter | solution.py:266
  889.1 4.0 copy-start.40
  (27 other events, 63.5 us)
Sparse Core Ops, SparseCore 0:
  9.7 118.4 all-gather.12
  129.8 44.0 all-gather.14
  175.5 148.2 all-gather.16
  325.2 147.8 all-gather.18
  532.7 42.0 reduce-scatter.6
  790.8 109.1 reduce-scatter.4
  902.5 144.9 reduce-scatter.10
  1050.0 145.2 reduce-scatter.8
where the time goes:
time: 1460 us; the launch traced here: 1450 us
  waiting for transfers between devices  483 us (33%)
  matrix products  384 us (26%)
  blocking collectives  362 us (25%)
  other arithmetic  124 us (8%)
  local copies, waits for them, and re-layouts  81.9 us (6%)
  between operations  16.5 us (1%)
    psum x1, blocking collectives, shards(): lax.psum((shares[0], shares[1], shares[2], shares[3], shares[4], shares[5...  250 us
    reduce_scatter x1, waiting for transfers between devices, shards(): lax.psum_scatter(up_grad.astype(jnp.bfloat16), 'shard', scatter_dimension...  148 us
    reduce_scatter x1, waiting for transfers between devices, shards(): lax.psum_scatter(down_grad.astype(jnp.bfloat16), 'shard', scatter_dimensi...  133 us
    all_gather x1, waiting for transfers between devices, shards(): lax.all_gather(w_down, 'shard', axis=0, tiled=True)  132 us
    dot_general x4, matrix products, block_scores(): jnp.einsum('qhd,khd->hqk', q_blk, keys, preferred_element_type=jnp.float32)  90.1 us
    dot_general x4, matrix products, right_dot(): lax.dot_general(left, right, (((1,), (1,)), ((), ())), preferred_element_...  56.9 us
    convert_element_type x2, other arithmetic, backward_block(): grad_scores = (probs * (grad_probs - inner)).astype(jnp.bfloat16)  54.8 us
    dot_general x4, matrix products, left_dot(): lax.dot_general(left, right, (((0,), (0,)), ((), ())), preferred_element_...  50.4 us
  transfers between devices with their start and end apart: 8, of which 5 were waited for; matrix products, arithmetic and copies ran while one was open for 36% of the time, Pallas kernels for 0%

commit v1 on v0

v1 whole, which is shorter than its diff:
```python
import functools

import jax
import jax.numpy as jnp
from jax import lax
from jax.experimental import pallas as pl
from jax.experimental.pallas import tpu as pltpu
from jax.sharding import PartitionSpec as P

HEADS = 16


EPS = 1e-05
GELU_C = 0.7978845608028654
GELU_A = 0.044715


def normalize(values):
    centred = values - jnp.mean(values, axis=-1, keepdims=True)
    scale = lax.rsqrt(jnp.mean(centred * centred, axis=-1, keepdims=True) + EPS)
    return (centred * scale, scale)


def norm_back(grad_h, normed, scale, gain):
    grad_n = grad_h * gain
    return scale * (
        grad_n
        - jnp.mean(grad_n, axis=-1, keepdims=True)
        - normed * jnp.mean(grad_n * normed, axis=-1, keepdims=True)
    )


def left_dot(left, right):
    return lax.dot_general(
        left, right, (((0,), (0,)), ((), ())), preferred_element_type=jnp.float32
    )


def right_dot(left, right):
    return lax.dot_general(
        left, right, (((1,), (1,)), ((), ())), preferred_element_type=jnp.float32
    )


def column_sum(values):
    return jnp.sum(values.astype(jnp.float32), axis=0)

GROUP = 8
MIB = 1 << 20


def peers():
    rep = lax.axis_index("rep")
    shard = lax.axis_index("shard")
    place = lax.rem(rep, GROUP)
    core = lax.rem(place, 2)
    east = lax.rem(place // 2, 2)
    north = place // 4
    return (
        rep,
        shard,
        (core, north, east),
        rep + 1 - 2 * core,
        rep + 2 - 4 * east,
        rep + 4 - 8 * north,
    )


def greet(count):
    rep, shard, _, core_peer, x_peer, y_peer = peers()
    barrier = pltpu.get_barrier_semaphore()
    for peer in (core_peer, x_peer, y_peer):
        pl.semaphore_signal(
            barrier, inc=1, device_id=(peer, shard), device_id_type=pl.DeviceIdType.MESH
        )
    for hop in range(1, count):
        pl.semaphore_signal(
            barrier,
            inc=1,
            device_id=(rep, lax.rem(shard + hop, count)),
            device_id_type=pl.DeviceIdType.MESH,
        )
    pl.semaphore_wait(barrier, 3 + count - 1)


def remote(source, target, send, recv, device):
    return pltpu.make_async_remote_copy(
        src_ref=source,
        dst_ref=target,
        send_sem=send,
        recv_sem=recv,
        device_id=device,
        device_id_type=pl.DeviceIdType.MESH,
    )


def gather_kernel(count, number, *refs):
    ins, outs = refs[:number], refs[number : 2 * number]
    send, recv, local = refs[2 * number :]
    rep, shard, (c, y, x), core_peer, x_peer, y_peer = peers()
    greet(count)
    started = {}
    owns = []
    hops = range(1, count)

    def owner(hop):
        return lax.rem(shard + count - hop, count)

    def push(m, stage, hop, source, target, device):
        copy = remote(
            source, target, send.at[m, stage, hop - 1], recv.at[m, stage, hop - 1], device
        )
        copy.start()
        started[m, stage, hop] = copy

    def step(m, stage):
        out = outs[m]
        half = out.shape[-1] // 2
        low, high = pl.ds(0, half), pl.ds(half, half)
        if stage == 0:
            for hop in hops:
                push(
                    m,
                    0,
                    hop,
                    ins[m].at[c, y, x],
                    out.at[shard, c, y, x],
                    (rep, lax.rem(shard + hop, count)),
                )
            own = pltpu.make_async_copy(ins[m], out.at[shard], local.at[m])
            own.start()
            owns.append(own)
        elif stage == 1:
            for hop in hops:
                started[m, 0, hop].wait_recv()
                s = owner(hop)
                first = out.at[s, c, y, x, :, low]
                second = out.at[s, c, y, x, :, high]
                push(m, 1, hop, first, first, (x_peer, shard))
                push(m, 2, hop, second, second, (y_peer, shard))
        elif stage == 2:
            for hop in hops:
                s = owner(hop)
                started[m, 1, hop].wait_recv()
                first = out.at[s, c, y, :, :, low]
                push(m, 3, hop, first, first, (y_peer, shard))
                started[m, 2, hop].wait_recv()
                second = out.at[s, c, :, x, :, high]
                push(m, 4, hop, second, second, (x_peer, shard))
        elif stage == 3:
            for hop in hops:
                s = owner(hop)
                started[m, 3, hop].wait_recv()
                started[m, 4, hop].wait_recv()
                push(m, 5, hop, out.at[s, c], out.at[s, c], (core_peer, shard))
        else:
            for hop in hops:
                started[m, 5, hop].wait_recv()

    for time in range(number + 4):
        for m in range(number):
            if 0 <= time - m <= 4:
                step(m, time - m)
    for copy in started.values():
        copy.wait_send()
    for own in owns:
        own.wait()


def gather_all(count, arrays):
    number = len(arrays)
    split = [a.reshape(2, 2, 2, a.shape[0] // GROUP, a.shape[1]) for a in arrays]
    outs = pl.pallas_call(
        functools.partial(gather_kernel, count, number),
        out_shape=[jax.ShapeDtypeStruct((count,) + a.shape, a.dtype) for a in split],
        in_specs=[pl.BlockSpec(memory_space=pl.ANY)] * number,
        out_specs=[pl.BlockSpec(memory_space=pl.ANY)] * number,
        scratch_shapes=[
            pltpu.SemaphoreType.DMA((number, 6, count - 1)),
            pltpu.SemaphoreType.DMA((number, 6, count - 1)),
            pltpu.SemaphoreType.DMA((number,)),
        ],
        compiler_params=pltpu.CompilerParams(
            collective_id=0, has_side_effects=True, vmem_limit_bytes=4 * MIB
        ),
        name="gather_parameters",
    )(*split)
    return [o.reshape(count * a.shape[0], a.shape[1]) for o, a in zip(outs, arrays)]


def add_into(target, source, lead, rows):
    chunk = 16

    def body(i, carry):
        at, sl = i // (rows // chunk), lax.rem(i, rows // chunk) * chunk
        sl = pl.ds(pl.multiple_of(sl, chunk), chunk)
        ref, index = target(at, sl)
        other, place = source(at, sl)
        ref[index] = (ref[index].astype(jnp.float32) + other[place].astype(jnp.float32)).astype(
            jnp.bfloat16
        )
        return carry

    lax.fori_loop(0, lead * (rows // chunk), body, 0)


def reduce_kernel(count, number, *refs):
    ins, outs = refs[:number], refs[number : 2 * number]
    scratch = refs[2 * number :]
    per = [scratch[7 * m : 7 * m + 7] for m in range(number)]
    send, recv, local = scratch[7 * number :]
    rep, shard, (c, y, x), core_peer, x_peer, y_peer = peers()
    greet(count)
    started = {}

    def push(m, k, source, target, device):
        copy = remote(source, target, send.at[m, k], recv.at[m, k], device)
        copy.start()
        started[m, k] = copy

    def step(m, stage):
        acc, r1, r2a, r2b, r3a, r3b, r4 = per[m]
        out = outs[m]
        rows, cols = acc.shape[-2:]
        half = cols // 2
        low, high = pl.ds(0, half), pl.ds(half, half)
        if stage == 0:
            push(m, 0, ins[m].at[:, 1 - c], r1, (core_peer, shard))
            own = pltpu.make_async_copy(ins[m].at[:, c], acc, local.at[m, 0])
            own.start()
            started[m, "own"] = own
        elif stage == 1:
            started[m, "own"].wait()
            started[m, 0].wait_recv()
            add_into(
                lambda i, sl: (acc, (i // 4, lax.rem(i // 2, 2), lax.rem(i, 2), sl)),
                lambda i, sl: (r1, (i // 4, lax.rem(i // 2, 2), lax.rem(i, 2), sl)),
                4 * count,
                rows,
            )
            push(m, 1, acc.at[:, 1 - y, :, :, low], r2a, (y_peer, shard))
            push(m, 2, acc.at[:, :, 1 - x, :, high], r2b, (x_peer, shard))
        elif stage == 2:
            started[m, 1].wait_recv()
            add_into(
                lambda i, sl: (acc, (i // 2, y, lax.rem(i, 2), sl, low)),
                lambda i, sl: (r2a, (i // 2, lax.rem(i, 2), sl)),
                2 * count,
                rows,
            )
            push(m, 3, acc.at[:, y, 1 - x, :, low], r3a, (x_peer, shard))
            started[m, 2].wait_recv()
            add_into(
                lambda i, sl: (acc, (i // 2, lax.rem(i, 2), x, sl, high)),
                lambda i, sl: (r2b, (i // 2, lax.rem(i, 2), sl)),
                2 * count,
                rows,
            )
            push(m, 4, acc.at[:, 1 - y, x, :, high], r3b, (y_peer, shard))
        elif stage == 3:
            started[m, 3].wait_recv()
            add_into(
                lambda i, sl: (acc, (i, y, x, sl, low)), lambda i, sl: (r3a, (i, sl)), count, rows
            )
            started[m, 4].wait_recv()
            add_into(
                lambda i, sl: (acc, (i, y, x, sl, high)), lambda i, sl: (r3b, (i, sl)), count, rows
            )
            for hop in range(1, count):
                to = lax.rem(shard + hop, count)
                push(m, 4 + hop, acc.at[to, y, x], r4.at[hop - 1], (rep, to))
        elif stage == 4:
            for hop in range(1, count):
                started[m, 4 + hop].wait_recv()

            def total(i, carry):
                sl = pl.ds(pl.multiple_of(i * 16, 16), 16)
                value = acc[shard, y, x, sl].astype(jnp.float32)
                for hop in range(1, count):
                    value = value + r4[hop - 1, sl].astype(jnp.float32)
                acc[shard, y, x, sl] = value.astype(jnp.bfloat16)
                return carry

            lax.fori_loop(0, rows // 16, total, 0)
            own = pltpu.make_async_copy(acc.at[shard, y, x], out.at[c, y, x], local.at[m, 1])
            own.start()
            started[m, "res"] = own
            k = 4 + count
            push(
                m, k, acc.at[shard, y, x, :, low], out.at[c, y, x, :, low], (x_peer, shard)
            )
            push(
                m, k + 1, acc.at[shard, y, x, :, high], out.at[c, y, x, :, high], (y_peer, shard)
            )
        elif stage == 5:
            k = 4 + count
            started[m, "res"].wait()
            started[m, k].wait_recv()
            first = out.at[c, y, :, :, low]
            push(m, k + 2, first, first, (y_peer, shard))
            started[m, k + 1].wait_recv()
            second = out.at[c, :, x, :, high]
            push(m, k + 3, second, second, (x_peer, shard))
        elif stage == 6:
            k = 4 + count
            started[m, k + 2].wait_recv()
            started[m, k + 3].wait_recv()
            push(m, k + 4, out.at[c], out.at[c], (core_peer, shard))
        else:
            started[m, 8 + count].wait_recv()

    for time in range(number + 7):
        for m in range(number):
            if 0 <= time - m <= 7:
                step(m, time - m)
    for (_, k), copy in started.items():
        if k not in ("own", "res"):
            copy.wait_send()


def reduce_all(count, arrays):
    number = len(arrays)
    split, scratch = [], []
    for a in arrays:
        rows, cols = a.shape[0] // (count * GROUP), a.shape[1]
        half = cols // 2
        split.append(a.reshape(count, 2, 2, 2, rows, cols))
        for shape in (
            (count, 2, 2, rows, cols),
            (count, 2, 2, rows, cols),
            (count, 2, rows, half),
            (count, 2, rows, half),
            (count, rows, half),
            (count, rows, half),
            (count - 1, rows, cols),
        ):
            scratch.append(pltpu.VMEM(shape, jnp.bfloat16))
    outs = pl.pallas_call(
        functools.partial(reduce_kernel, count, number),
        out_shape=[jax.ShapeDtypeStruct(a.shape[1:], a.dtype) for a in split],
        in_specs=[pl.BlockSpec(memory_space=pl.ANY)] * number,
        out_specs=[pl.BlockSpec(memory_space=pl.ANY)] * number,
        scratch_shapes=scratch
        + [
            pltpu.SemaphoreType.DMA((number, 9 + count)),
            pltpu.SemaphoreType.DMA((number, 9 + count)),
            pltpu.SemaphoreType.DMA((number, 2)),
        ],
        compiler_params=pltpu.CompilerParams(
            collective_id=1, has_side_effects=True, vmem_limit_bytes=48 * MIB
        ),
        name="reduce_gradients",
    )(*split)
    return [o.reshape(a.shape[0] // count, a.shape[1]) for o, a in zip(outs, arrays)]


def slope_of(heads, head):
    return jnp.exp2(jnp.full((1, 1), -8.0 / heads, jnp.float32) * (head + 1).astype(jnp.float32))


def set_distance(dist_ref, seg_row, seg_col):
    rows = dist_ref.shape[0]
    for start in range(0, rows, BLOCK):
        shape = (rows, BLOCK)
        key = lax.broadcasted_iota(jnp.int32, shape, 0)
        query = lax.broadcasted_iota(jnp.int32, shape, 1) + start
        allowed = (key <= query) & (seg_col[...] == seg_row[:, pl.ds(start, BLOCK)])
        dist_ref[:, pl.ds(start, BLOCK)] = jnp.where(
            allowed, (key - query).astype(jnp.float32), -1e30
        )


BLOCK = 256


def own_half(values, side, axis):
    place = lax.broadcasted_iota(jnp.int32, values.shape, axis)
    mine = (place < 64) if side == 0 else (place >= 64)
    return jnp.where(mine, values, jnp.zeros_like(values))


def scores_of(q_half, keys, dist, slope):
    raw = lax.dot_general(
        keys, q_half, (((1,), (1,)), ((), ())), preferred_element_type=jnp.float32
    )
    return raw + slope * dist


def attend_kernel(heads, seg_row, seg_col, q_ref, k_ref, v_ref, mixed_ref, lse_ref, dist_ref):
    rows, width = q_ref.shape
    step = pl.program_id(0)

    @pl.when(step == 0)
    def _():
        set_distance(dist_ref, seg_row, seg_col)

    for start in range(0, rows, BLOCK):
        seen = start + BLOCK
        at = pl.ds(start, BLOCK)
        query = q_ref[at, :] * jnp.bfloat16(0.125)
        parts = []
        for side in range(2):
            slope = slope_of(heads, step * 2 + side)
            scores = scores_of(
                own_half(query, side, 1), k_ref[0:seen, :], dist_ref[0:seen, at], slope
            )
            top = jnp.max(scores, axis=0, keepdims=True)
            weights = jnp.exp(scores - top)
            total = jnp.sum(weights, axis=0, keepdims=True)
            lse_ref[0, pl.ds(side, 1), at] = top + jnp.log(total)
            value = left_dot(v_ref[0:seen, :], weights.astype(jnp.bfloat16)) / total
            parts.append(value[side * 64 : side * 64 + 64])
        mixed_ref[at, :] = jnp.concatenate(parts, axis=0).T.astype(jnp.bfloat16)


def attend_back_kernel(
    heads,
    seg_row,
    seg_col,
    q_ref,
    k_ref,
    v_ref,
    gm_ref,
    lse_ref,
    gq_ref,
    gk_ref,
    gv_ref,
    dist_ref,
    sum_k,
    sum_v,
):
    rows, width = q_ref.shape
    step = pl.program_id(0)

    @pl.when(step == 0)
    def _():
        set_distance(dist_ref, seg_row, seg_col)

    for start in range(rows - BLOCK, -1, -BLOCK):
        seen = start + BLOCK
        at = pl.ds(start, BLOCK)
        query = q_ref[at, :] * jnp.bfloat16(0.125)
        grad = gm_ref[at, :]
        parts = []
        add_k = jnp.zeros((seen, width), jnp.float32)
        add_v = jnp.zeros((seen, width), jnp.float32)
        for side in range(2):
            slope = slope_of(heads, step * 2 + side)
            q_half = own_half(query, side, 1)
            g_half = own_half(grad, side, 1)
            scores = scores_of(q_half, k_ref[0:seen, :], dist_ref[0:seen, at], slope)
            probs = jnp.exp(scores - lse_ref[0, pl.ds(side, 1), at])
            grad_probs = right_dot(v_ref[0:seen, :], g_half)
            inner = jnp.sum(probs * grad_probs, axis=0, keepdims=True)
            grad_scores = (probs * (grad_probs - inner)).astype(jnp.bfloat16)
            value = left_dot(k_ref[0:seen, :], grad_scores) * 0.125
            parts.append(value[side * 64 : side * 64 + 64])
            add_k = add_k + jnp.dot(grad_scores, q_half, preferred_element_type=jnp.float32)
            add_v = add_v + jnp.dot(
                probs.astype(jnp.bfloat16), g_half, preferred_element_type=jnp.float32
            )
        gq_ref[at, :] = jnp.concatenate(parts, axis=0).T.astype(jnp.bfloat16)
        if seen == rows:
            sum_k[...] = add_k
            sum_v[...] = add_v
        else:
            sum_k[0:seen, :] += add_k
            sum_v[0:seen, :] += add_v
    gk_ref[...] = sum_k[...].astype(jnp.bfloat16)
    gv_ref[...] = sum_v[...].astype(jnp.bfloat16)


def attend(qkv, segments):
    rows, width = qkv.shape[0], qkv.shape[1] // 3
    pairs = width // 128
    return pl.pallas_call(
        functools.partial(attend_kernel, HEADS),
        grid=(pairs,),
        in_specs=[
            pl.BlockSpec((1, rows), lambda i: (0, 0)),
            pl.BlockSpec((rows, 1), lambda i: (0, 0)),
            pl.BlockSpec((rows, 128), lambda i: (0, i)),
            pl.BlockSpec((rows, 128), lambda i: (0, i + pairs)),
            pl.BlockSpec((rows, 128), lambda i: (0, i + 2 * pairs)),
        ],
        out_specs=[
            pl.BlockSpec((rows, 128), lambda i: (0, i)),
            pl.BlockSpec((1, 2, rows), lambda i: (i, 0, 0)),
        ],
        out_shape=[
            jax.ShapeDtypeStruct((rows, width), jnp.bfloat16),
            jax.ShapeDtypeStruct((pairs, 2, rows), jnp.float32),
        ],
        scratch_shapes=[pltpu.VMEM((rows, rows), jnp.float32)],
        compiler_params=pltpu.CompilerParams(vmem_limit_bytes=40 * MIB),
        name="attend",
    )(segments, segments.reshape(rows, 1), qkv, qkv, qkv)


def attend_back(qkv, segments, grad_mixed, lse):
    rows, width = grad_mixed.shape
    pairs = width // 128
    block = pl.BlockSpec((rows, 128), lambda i: (0, i))
    return pl.pallas_call(
        functools.partial(attend_back_kernel, HEADS),
        grid=(pairs,),
        in_specs=[
            pl.BlockSpec((1, rows), lambda i: (0, 0)),
            pl.BlockSpec((rows, 1), lambda i: (0, 0)),
            block,
            pl.BlockSpec((rows, 128), lambda i: (0, i + pairs)),
            pl.BlockSpec((rows, 128), lambda i: (0, i + 2 * pairs)),
            block,
            pl.BlockSpec((1, 2, rows), lambda i: (i, 0, 0)),
        ],
        out_specs=[block, block, block],
        out_shape=[jax.ShapeDtypeStruct((rows, width), jnp.bfloat16)] * 3,
        scratch_shapes=[
            pltpu.VMEM((rows, rows), jnp.float32),
            pltpu.VMEM((rows, 128), jnp.float32),
            pltpu.VMEM((rows, 128), jnp.float32),
        ],
        compiler_params=pltpu.CompilerParams(vmem_limit_bytes=40 * MIB),
        name="attend_back",
    )(segments, segments.reshape(rows, 1), qkv, qkv, qkv, grad_mixed, lse)


def pack(pieces, shape):
    joined = jnp.concatenate([p.astype(jnp.bfloat16) for p in pieces], axis=-1)
    room = shape[-2] * shape[-1] - joined.shape[-1]
    pad = [(0, 0)] * (joined.ndim - 1) + [(0, room)]
    return jnp.pad(joined, pad).reshape((-1, shape[-1]))


def unpack(packed, count, sizes):
    flat = packed.reshape(count, -1)
    out, at = [], 0
    for size in sizes:
        out.append(flat[:, at : at + size].reshape(-1))
        at += size
    return out


def shards(
    tokens,
    segments,
    ln1_gain,
    ln1_bias,
    w_qkv,
    q_bias,
    v_bias,
    w_out,
    out_bias,
    ln2_gain,
    ln2_bias,
    w_up,
    up_bias,
    w_down,
    down_bias,
    cotangent,
):
    count = lax.axis_size("shard")
    vectors = (
        ln1_gain,
        ln1_bias,
        q_bias,
        v_bias,
        out_bias,
        ln2_gain,
        ln2_bias,
        down_bias,
        up_bias,
    )
    sizes = [v.shape[0] for v in vectors]
    small_rows = -(-sum(sizes) // (256 * 128)) * 128
    small = (small_rows, 256)
    small_full, qkv_matrix, out_matrix, up_matrix, down_matrix = gather_all(
        count, [pack(vectors, small), w_qkv, w_out, w_up, w_down]
    )
    (
        first_gain,
        first_shift,
        query_bias,
        value_bias,
        out_shift,
        second_gain,
        second_shift,
        down_shift,
        up_shift,
    ) = unpack(small_full, count, sizes)
    rows, width = tokens.shape
    inputs = tokens.astype(jnp.float32)
    normed_one, scale_one = normalize(inputs)
    first = (normed_one * first_gain.astype(jnp.float32) + first_shift.astype(jnp.float32)).astype(
        jnp.bfloat16
    )
    joined = jnp.concatenate([query_bias, jnp.zeros_like(query_bias), value_bias]).astype(
        jnp.float32
    )
    qkv = (jnp.dot(first, qkv_matrix, preferred_element_type=jnp.float32) + joined).astype(
        jnp.bfloat16
    )
    mixed, lse = attend(qkv, segments)
    middle = (
        inputs
        + jnp.dot(mixed, out_matrix, preferred_element_type=jnp.float32)
        + out_shift.astype(jnp.float32)
    )
    normed_two, scale_two = normalize(middle)
    second = (
        normed_two * second_gain.astype(jnp.float32) + second_shift.astype(jnp.float32)
    ).astype(jnp.bfloat16)
    upper = jnp.dot(second, up_matrix, preferred_element_type=jnp.float32) + up_shift.astype(
        jnp.float32
    )
    tanh_value = jnp.tanh(GELU_C * (upper + GELU_A * upper * upper * upper))
    active = (0.5 * upper * (1.0 + tanh_value)).astype(jnp.bfloat16)
    output = (
        middle
        + jnp.dot(active, down_matrix, preferred_element_type=jnp.float32)
        + down_shift.astype(jnp.float32)
    ).astype(jnp.bfloat16)
    down_shift_grad = column_sum(cotangent)
    down_grad = left_dot(active, cotangent)
    grad_active = right_dot(cotangent, down_matrix)
    gelu_slope = 0.5 * (1.0 + tanh_value) + 0.5 * upper * (
        1.0 - tanh_value * tanh_value
    ) * GELU_C * (1.0 + 3.0 * GELU_A * upper * upper)
    grad_upper = (grad_active * gelu_slope).astype(jnp.bfloat16)
    up_shift_grad = column_sum(grad_upper)
    up_grad = left_dot(second, grad_upper)
    grad_second = right_dot(grad_upper, up_matrix)
    second_gain_grad = jnp.sum(grad_second * normed_two, axis=0)
    second_shift_grad = jnp.sum(grad_second, axis=0)
    grad_middle = cotangent.astype(jnp.float32) + norm_back(
        grad_second, normed_two, scale_two, second_gain.astype(jnp.float32)
    )
    grad_branch = grad_middle.astype(jnp.bfloat16)
    out_shift_grad = column_sum(grad_branch)
    out_grad = left_dot(mixed, grad_branch)
    grad_mixed = right_dot(grad_branch, out_matrix).astype(jnp.bfloat16)
    grad_qkv = jnp.concatenate(attend_back(qkv, segments, grad_mixed, lse), axis=1)
    query_bias_grad = column_sum(grad_qkv[:, :width])
    value_bias_grad = column_sum(grad_qkv[:, 2 * width :])
    qkv_grad = left_dot(first, grad_qkv)
    grad_first = right_dot(grad_qkv, qkv_matrix)
    first_gain_grad = jnp.sum(grad_first * normed_one, axis=0)
    first_shift_grad = jnp.sum(grad_first, axis=0)
    token_grad = (
        grad_middle + norm_back(grad_first, normed_one, scale_one, first_gain.astype(jnp.float32))
    ).astype(jnp.bfloat16)
    grads = (
        first_gain_grad,
        first_shift_grad,
        query_bias_grad,
        value_bias_grad,
        out_shift_grad,
        second_gain_grad,
        second_shift_grad,
        down_shift_grad,
        up_shift_grad,
    )
    packed = pack([g.reshape(count, -1) for g in grads], small)
    shares = reduce_all(
        count,
        [
            down_grad.astype(jnp.bfloat16),
            up_grad.astype(jnp.bfloat16),
            out_grad.astype(jnp.bfloat16),
            qkv_grad.astype(jnp.bfloat16),
            packed,
        ],
    )
    shares = [share.astype(jnp.float32) for share in shares]
    groups = lax.axis_size("rep") // GROUP
    if groups > 1:
        shares = [share / GROUP for share in lax.psum(shares, "rep")]
    down_sum, up_sum, out_sum, qkv_sum, small_sum = shares
    (
        ln1_gain_sum,
        ln1_bias_sum,
        q_bias_sum,
        v_bias_sum,
        out_bias_sum,
        ln2_gain_sum,
        ln2_bias_sum,
        down_bias_sum,
        up_bias_sum,
    ) = unpack(small_sum, 1, sizes)
    return (
        output,
        token_grad,
        ln1_gain_sum,
        ln1_bias_sum,
        qkv_sum,
        q_bias_sum,
        v_bias_sum,
        out_sum,
        out_bias_sum,
        ln2_gain_sum,
        ln2_bias_sum,
        up_sum,
        up_bias_sum,
        down_sum,
        down_bias_sum,
    )


def solution(mesh):
    in_specs = (
        P(("rep", "shard"), None),
        P(("rep", "shard"), None),
        P("shard"),
        P("shard"),
        P("shard", None),
        P("shard"),
        P("shard"),
        P("shard", None),
        P("shard"),
        P("shard"),
        P("shard"),
        P("shard", None),
        P("shard"),
        P("shard", None),
        P("shard"),
        P(("rep", "shard"), None),
    )
    out_specs = (
        P(("rep", "shard"), None),
        P(("rep", "shard"), None),
        P("shard"),
        P("shard"),
        P("shard", None),
        P("shard"),
        P("shard"),
        P("shard", None),
        P("shard"),
        P("shard"),
        P("shard"),
        P("shard", None),
        P("shard"),
        P("shard", None),
        P("shard"),
    )
    return jax.shard_map(shards, mesh=mesh, in_specs=in_specs, out_specs=out_specs, check_vma=False)
```

time: 1460 us -> 598 us (0.41)
  waiting for transfers between devices: 483 us -> 0 us
  blocking collectives: 362 us -> 0 us
  Pallas kernels: 0 us -> 358 us
  matrix products: 384 us -> 141 us
  other arithmetic: 124 us -> 36 us
  local copies, waits for them, and re-layouts: 81.9 us -> 54.8 us
  between operations: 16.5 us -> 1.67 us
    pallas_call x0 -> x4, Pallas kernels: none -> 358 us  [the longest x1 174 us: reduce_all(): pl.pallas_call(functools.partial(reduce_kernel, count, number), out_shape...]
    reduce_scatter x4 -> x0, waiting for transfers between devices: 281 us -> none  [the longest x1 148 us: shards(): lax.psum_scatter(up_grad.astype(jnp.bfloat16), 'shard', scatter_dimension...]
    psum x1 -> x0, blocking collectives: 250 us -> none  [shards(): lax.psum((shares[0], shares[1], shares[2], shares[3], shares[4], shares[5...]
    dot_general x14 -> x0, matrix products: 227 us -> none  [the longest x4 90.1 us: block_scores(): jnp.einsum('qhd,khd->hqk', q_blk, keys, preferred_element_type=jnp.float32)]
    all_gather x4 -> x0, waiting for transfers between devices: 199 us -> none  [the longest x1 132 us: shards(): lax.all_gather(w_down, 'shard', axis=0, tiled=True)]
    all_gather x9 -> x0, blocking collectives: 91.4 us -> none  [the longest x1 15.8 us: shards(): lax.all_gather(up_bias, 'shard', axis=0, tiled=True)]
    convert_element_type x23 -> x4, other arithmetic: 61.3 us -> 9.84 us  [shards(): shares = [share.astype(jnp.float32) for share in shares]]
    reduce_sum x2 -> x0, other arithmetic: 33.4 us -> none  [forward_block(): total = jnp.sum(weights, axis=-1, keepdims=True)]
  transfers between devices with their start and end apart: 8 -> 0, of which waited for: 5 -> 0; matrix products, arithmetic and copies ran while one was open for 36% -> 0% of each run, Pallas kernels for 0% -> 0%
where the time goes in v1:
time: 598 us; the launch traced here: 591 us
  Pallas kernels  358 us (60%)
  matrix products  141 us (24%)
  local copies, waits for them, and re-layouts  54.8 us (9%)
  other arithmetic  36 us (6%)
    pallas_call x1, Pallas kernels, reduce_all(): pl.pallas_call(functools.partial(reduce_kernel, count, number), out_shape...  174 us
    pallas_call x1, Pallas kernels, gather_all(): pl.pallas_call(functools.partial(gather_kernel, count, number), out_shape...  101 us
    dot_general x4, matrix products, right_dot(): lax.dot_general(left, right, (((1,), (1,)), ((), ())), preferred_element_...  51.4 us
    pallas_call x1, Pallas kernels, attend_back(): pl.pallas_call(functools.partial(attend_back_kernel, HEADS), grid=(pairs,...  47.2 us
    dot_general x4, matrix products, left_dot(): lax.dot_general(left, right, (((0,), (0,)), ((), ())), preferred_element_...  47.2 us
    unnamed x106, local copies, waits for them, and re-layouts  41.3 us
    pallas_call x1, Pallas kernels, attend(): pl.pallas_call(functools.partial(attend_kernel, HEADS), grid=(pairs,), in...  35.8 us
    dot_general x1, matrix products, shards(): jnp.dot(active, down_matrix, preferred_element_type=jnp.float32)  16.9 us

profile of v1, /device:TPU:0, one launch (start us, length us, event | category | flops | bytes accessed | tf_op | source)
XLA Modules:
  0.0 590.7 jit_solution(9623822819975780140)
XLA Ops:
  13.7 100.9 %gather_parameters.1 = (bf16[4,2,2,2,16,256]{5,4,3,2,1,0:T(8,128)(2,1)S(1)}, bf16[4,2,2,2,32,3072]{5,4,3,2,1,0:T(8,128)(2,1)S(1)}, bf16[4,2,2,2,32,1024]{5,4,3,2...) custom-call(bf16[2,2,2,16,256]{4,3,2,1,0:T(8,128)(2,1)S(1)} %reshape_reshape.9.refs, ...), custom_call_target="tpu_custom_call" | custom-call | tf_op jit(solution)/shard_map/gather_parameters/pallas_call | solution.py:173
  114.7 3.2 copy-done.7
  117.9 3.2 copy-done.8
  121.1 2.7 copy-done.9
  124.3 3.9 copy.40
  132.7 10.3 %add_convert_fusion.q_ref.k_ref.v_ref = bf16[1024,3072]{1,0:T(8,128)(2,1)S(1)} fusion(f32[3072]{0:T(1024)S(1)} %maximum_convert_fusion, bf16[1024,3072]{1,0:T(8,128)(2,1)} %bitcast.102, bf16[1024,1024]{0,1:T(8,128)(2,1)S(1)} %copy-done.12, f32[1024]{0:T(1024)S(1)} %bitcast.130, f32[1024]{0:T(1024)S(1)} %bitcast.117, f32[1024]{0:T(1024)S(1)} %add_rsqrt_fusion.1, ...), kind=kOutput, calls=%fused_computation.10 | convolution fusion | flops 6455033856 | bytes 14708736 | tf_op jit(solution)/shard_map/dot_general | solution.py:600
  143.0 35.8 %attend.1 = (bf16[1024,1024]{1,0:T(8,128)(2,1)S(1)}, f32[8,2,1024]{2,1,0:T(2,128)S(1)}) custom-call(s32[1,1024]{1,0:T(1,128)S(1)} %copy-done.6, s32[1024,1]{1,0:T(8,128)S(1)} %copy.41.seg_col, bf16[1024,3072]{1,0:T(8,128)(2,1)S(1)} %add_convert_fusion.q_ref.k_ref.v_ref, bf16[1024,3072]{1,0:T(8,128)(2,1)S(1)} %add_convert_fusion.q_ref.k_ref.v_ref, ...), custom_call_target="tpu_custom_call" | custom-call | tf_op jit(solution)/shard_map/attend/pallas_call | solution.py:476
  178.9 2.6 fusion.31
  184.4 12.3 %fusion.27 = f32[1024,4096]{1,0:T(8,128)} fusion(bf16[1024,4096]{1,0:T(8,128)(2,1)S(1)} %bitcast.99, f32[1024,1024]{0,1:T(8,128)S(1)} %get-tuple-element.104, f32[1024]{0:T(1024)S(1)} %bitcast.132, f32[1024]{0:T(1024)S(1)} %bitcast.121, f32[1024]{0:T(1024)S(1)} %add_rsqrt_fusion, f32[1024]{0:T(1024)S(1)} %broadcast_multiply_fusion.4), kind=kOutput, calls=%fused_computation.83 | convolution fusion | flops 8595177472 | bytes 29376512 | tf_op jit(solution)/shard_map/dot_general | solution.py:613
  196.6 16.9 %add_convert_fusion.1 = bf16[1024,1024]{0,1:T(8,128)(2,1)} fusion(f32[1024,1024]{0,1:T(8,128)} %copy-done.14, f32[1024]{0:T(1024)S(1)} %bitcast.136, bf16[4096,1024]{1,0:T(8,128)(2,1)} %bitcast.100, f32[1024,4096]{1,0:T(8,128)} %fusion.27, f32[4096]{0:T(1024)S(1)} %bitcast.125), kind=kOutput, calls=%fused_computation.36 | convolution fusion | flops 8635023360 | bytes 31477760 | tf_op jit(solution)/shard_map/dot_general | solution.py:620
  213.5 3.9 copy.49
  217.5 25.4 %fusion.34 = (bf16[4096]{0:T(1024)(128)(2,1)S(1)}, bf16[1024,4096]{1,0:T(8,128)(2,1)}) fusion(f32[1024,4096]{1,0:T(8,128)} %fusion.27, f32[4096]{0:T(1024)S(1)} %bitcast.126, bf16[4096,1024]{1,0:T(8,128)(2,1)} %bitcast.101, bf16[1024,1024]{1,0:T(8,128)(2,1)} %param.31), kind=kOutput, calls=%fused_computation.90 | convolution fusion | flops 8678010880 | bytes 35676160 | tf_op jit(solution)/shard_map/dot_general | solution.py:40
  242.9 15.1 %fusion.33 = (bf16[1024]{0:T(1024)(128)(2,1)S(1)}, f32[1024,1024]{1,0:T(8,128)}) fusion(bf16[1024,4096]{1,0:T(8,128)(2,1)} %get-tuple-element.110, bf16[1024,4096]{1,0:T(8,128)(2,1)} %bitcast.96), kind=kOutput, calls=%fused_computation.89 | convolution fusion | flops 8590982144 | bytes 20973568 | tf_op jit(solution)/shard_map/dot_general | solution.py:40
  257.9 5.5 copy.44
  263.4 4.3 multiply_reduce_fusion
  267.7 3.9 copy.43
  271.7 5.0 convert_reduce_fusion.1
  276.7 2.4 convolution_convert_fusion.4.gm_ref
  279.2 47.2 %attend_back.1 = (bf16[1024,1024]{1,0:T(8,128)(2,1)S(1)}, bf16[1024,1024]{1,0:T(8,128)(2,1)S(1)}, bf16[1024,1024]{1,0:T(8,128)(2,1)S(1)}) custom-call(s32[1,1024]{1,0:T(1,128)S(1)} %copy-done.6, s32[1024,1]{1,0:T(8,128)S(1)} %copy.41.seg_col, bf16[1024,3072]{1,0:T(8,128)(2,1)} %copy-done, bf16[1024,3072]{1,0:T(8,128)(2,1)} %copy-done, ...), custom_call_target="tpu_custom_call" | custom-call | tf_op jit(solution)/shard_map/attend_back/pallas_call | solution.py:504
  328.0 8.5 %fusion.32 = (bf16[1024]{0:T(1024)(128)(2,1)S(1)}, f32[1024,1024]{1,0:T(8,128)}) fusion(bf16[1024,3072]{1,0:T(8,128)(2,1)S(1)} %get-tuple-element.84, bf16[1024,3072]{1,0:T(8,128)(2,1)S(1)} %bitcast.105), kind=kOutput, calls=%fused_computation.88 | convolution fusion | flops 6443498496 | bytes 16779264 | tf_op jit(solution)/shard_map/dot_general | solution.py:40
  336.5 5.5 copy.46
  342.1 3.7 fusion.20
  345.8 4.9 fusion.19
  350.7 3.9 copy.50
  354.7 19.0 %convolution_convert_fusion.1 = bf16[4096,1024]{1,0:T(8,128)(2,1)} fusion(bf16[1024,1024]{1,0:T(8,128)(2,1)} %param.31, f32[1024,4096]{1,0:T(8,128)} %fusion.27, f32[4096]{0:T(1024)S(1)} %bitcast.127), kind=kOutput, calls=%fused_computation.12 | convolution fusion | flops 8636071936 | bytes 27279360 | tf_op jit(solution)/shard_map/dot_general | solution.py:34
  373.7 15.3 %convolution_convert_fusion = bf16[1024,4096]{1,0:T(8,128)(2,1)} fusion(bf16[1024,4096]{1,0:T(8,128)(2,1)} %get-tuple-element.110, f32[1024,1024]{0,1:T(8,128)S(1)} %copy-done.15, f32[1024]{0:T(1024)S(1)} %bitcast.133, f32[1024]{0:T(1024)S(1)} %bitcast.124, f32[1024]{0:T(1024)S(1)} %add_rsqrt_fusion, f32[1024]{0:T(1024)S(1)} %broadcast_multiply_fusion.4), kind=kOutput, calls=%fused_computation.11 | convolution fusion | flops 8599371776 | bytes 20987904 | tf_op jit(solution)/shard_map/dot_general | solution.py:34
  389.0 3.7 convolution_convert_fusion.3
  392.7 9.2 %convolution_convert_fusion.2 = bf16[1024,3072]{1,0:T(8,128)(2,1)} fusion(bf16[1024,3072]{1,0:T(8,128)(2,1)S(1)} %bitcast.114, bf16[1024,1024]{0,1:T(8,128)(2,1)S(1)} %copy-done.13, f32[1024]{0:T(1024)S(1)} %bitcast.131, f32[1024]{0:T(1024)S(1)} %bitcast.120, f32[1024]{0:T(1024)S(1)} %copy-done.26, f32[1024]{0:T(1024)S(1)} %copy-done.22), kind=kOutput, calls=%fused_computation.16 | convolution fusion | flops 6451888128 | bytes 14696448 | tf_op jit(solution)/shard_map/dot_general | solution.py:34
  404.2 173.7 %reduce_gradients.1 = (bf16[2,2,2,128,1024]{4,3,2,1,0:T(8,128)(2,1)S(1)}, bf16[2,2,2,32,4096]{4,3,2,1,0:T(8,128)(2,1)}, bf16[2,2,2,32,1024]{4,3,2,1,0:T(8,128)(2...) custom-call(bf16[4,2,2,2,128,1024]{5,4,3,2,1,0:T(8,128)(2,1)} %bitcast.108, ...), custom_call_target="tpu_custom_call" | custom-call | tf_op jit(solution)/shard_map/reduce_gradients/pallas_call | solution.py:338
  579.8 3.5 bitcast_convert_fusion.2
  584.4 2.6 bitcast_convert_fusion.1
  587.6 2.6 bitcast_convert_fusion
  (139 shorter events, 28.2 us)
Async XLA Ops:
  0.6 123.4 %copy-start.6 = (s32[1,1024]{1,0:T(1,128)S(1)}, s32[1,1024]{1,0:T(1,128)}, u32[]{:S(2)}) copy-start(s32[1,1024]{1,0:T(1,128)} %seg_row.3) | copy-start | bytes 12292
  8.1 1.6 copy-start.1
  114.7 3.2 copy-start.7
  117.9 3.2 copy-start.8
  121.1 2.7 copy-start.9
  128.3 4.4 copy-start.12
  128.3 4.4 copy-start.27
  128.3 14.7 %copy-start.23 = (f32[1,2,4,128]{3,1,2,0:T(2,128)}, f32[1,2,4,128]{3,1,2,0:T(2,128)S(1)}, u32[]{:S(2)}) copy-start(f32[1,2,4,128]{3,1,2,0:T(2,128)S(1)} %copy.53) | copy-start | bytes 12292
  130.4 12.6 %copy-start.21 = (f32[1024]{0:T(1024)}, f32[1024]{0:T(1024)S(1)}, u32[]{:S(2)}) copy-start(f32[1024]{0:T(1024)S(1)} %broadcast_multiply_fusion.5) | copy-start | bytes 12292
  132.7 10.3 %copy-start.25 = (f32[1024]{0:T(1024)}, f32[1024]{0:T(1024)S(1)}, u32[]{:S(2)}) copy-start(f32[1024]{0:T(1024)S(1)} %add_rsqrt_fusion.1) | copy-start | bytes 12292
  143.0 35.8 %copy-start = (bf16[1024,3072]{1,0:T(8,128)(2,1)}, bf16[1024,3072]{1,0:T(8,128)(2,1)S(1)}, u32[]{:S(2)}) copy-start(bf16[1024,3072]{1,0:T(8,128)(2,1)S(1)} %add_convert_fusion.q_ref.k_ref.v_ref) | copy-start | bytes 18874372
  178.8 2.7 copy-start.10
  178.8 3.6 slice-start
  178.8 5.5 slice-start.1
  181.5 15.1 %copy-start.14 = (f32[1024,1024]{0,1:T(8,128)}, f32[1024,1024]{0,1:T(8,128)S(1)}, u32[]{:S(2)}) copy-start(f32[1024,1024]{0,1:T(8,128)S(1)} %get-tuple-element.104) | copy-start | bytes 12582916
  276.7 2.4 copy-start.17
  276.7 51.2 %slice-start.2 = ((s8[6291456]{0:T(1024)(128)(4,1)}), s8[4194304]{0:T(1024)(128)(4,1)S(1)}, s32[]{:S(2)}) async-start(s8[6291456]{0:T(1024)(128)(4,1)} %bitcast.103), calls=%async_computation.2 | async-start | bytes 8388608
  279.2 48.8 %slice-start.3 = ((s8[6291456]{0:T(1024)(128)(4,1)}), s8[2097152]{0:T(1024)(128)(4,1)S(1)}, s32[]{:S(2)}) async-start(s8[6291456]{0:T(1024)(128)(4,1)} %bitcast.103), calls=%async_computation.3 | async-start | bytes 4194304
  327.9 8.6 %copy-start.20 = (bf16[1024,3072]{1,0:T(8,128)(2,1)}, bf16[1024,3072]{1,0:T(8,128)(2,1)S(1)}, u32[]{:S(2)}) copy-start(bf16[1024,3072]{1,0:T(8,128)(2,1)S(1)} %get-tuple-element.84) | copy-start | bytes 18874372
  336.5 5.5 copy-start.13
  336.5 5.5 copy-start.22
  336.5 5.5 copy-start.24
  336.5 5.5 copy-start.26
  342.1 3.8 copy-start.16
  354.7 19.0 %copy-start.15 = (f32[1024,1024]{0,1:T(8,128)S(1)}, f32[1024,1024]{0,1:T(8,128)}, u32[]{:S(2)}) copy-start(f32[1024,1024]{0,1:T(8,128)} %copy-done.14) | copy-start | bytes 12582916
  354.7 19.0 %copy-start.30 = (f32[1,2,4,128]{3,1,2,0:T(2,128)S(1)}, f32[1,2,4,128]{3,1,2,0:T(2,128)}, u32[]{:S(2)}) copy-start(f32[1,2,4,128]{3,1,2,0:T(2,128)} %copy-done.29) | copy-start | bytes 12292
  354.7 38.0 %slice-start.4 = ((s8[6291456]{0:T(1024)(128)(4,1)}), s8[4194304]{0:T(1024)(128)(4,1)S(1)}, s32[]{:S(2)}) async-start(s8[6291456]{0:T(1024)(128)(4,1)} %bitcast.113), calls=%async_computation.4 | async-start | bytes 8388608
  373.6 15.3 %copy-start.11 = (bf16[1024,1024]{1,0:T(8,128)(2,1)S(1)}, bf16[1024,1024]{1,0:T(8,128)(2,1)}, u32[]{:S(2)}) copy-start(bf16[1024,1024]{1,0:T(8,128)(2,1)} %copy-done.10) | copy-start | bytes 6291460
  373.6 15.3 %copy-start.18 = (f32[1024,1024]{0,1:T(8,128)S(1)}, f32[1024,1024]{0,1:T(8,128)}, u32[]{:S(2)}) copy-start(f32[1024,1024]{0,1:T(8,128)} %copy-done.17) | copy-start | bytes 12582916
  373.7 19.0 %slice-start.5 = ((s8[6291456]{0:T(1024)(128)(4,1)}), s8[2097152]{0:T(1024)(128)(4,1)S(1)}, s32[]{:S(2)}) async-start(s8[6291456]{0:T(1024)(128)(4,1)} %bitcast.113), calls=%async_computation.5 | async-start | bytes 4194304
  389.0 3.7 copy-start.28
  579.2 5.2 copy-start.19
  (5 other events, 6.1 us)

commit v2 on v1

--- a/solution.py
+++ b/solution.py
@@ -4,6 +4,7 @@
 import jax.numpy as jnp
 from jax import lax
 from jax.experimental import pallas as pl
+from jax.experimental.layout import Layout, with_layout_constraint
 from jax.experimental.pallas import tpu as pltpu
 from jax.sharding import PartitionSpec as P
 
@@ -40,6 +41,10 @@
     return lax.dot_general(
         left, right, (((1,), (1,)), ((), ())), preferred_element_type=jnp.float32
     )
+
+
+def by_rows(values):
+    return with_layout_constraint(values, Layout((0, 1)))
 
 
 def column_sum(values):
@@ -83,6 +88,17 @@
     pl.semaphore_wait(barrier, 3 + count - 1)
 
 
+CHUNK = 2 << 20
+
+
+def cut(shapes):
+    chunks = []
+    for a, (rows, cols) in enumerate(shapes):
+        parts = max(1, rows * cols // CHUNK)
+        chunks += [(a, k * (cols // parts), cols // parts) for k in range(parts)]
+    return chunks
+
+
 def remote(source, target, send, recv, device):
     return pltpu.make_async_remote_copy(
         src_ref=source,
@@ -94,7 +110,7 @@
     )
 
 
-def gather_kernel(count, number, *refs):
+def gather_kernel(count, number, chunks, *refs):
     ins, outs = refs[:number], refs[number : 2 * number]
     send, recv, local = refs[2 * number :]
     rep, shard, (c, y, x), core_peer, x_peer, y_peer = peers()
@@ -114,22 +130,25 @@
         started[m, stage, hop] = copy
 
     def step(m, stage):
-        out = outs[m]
-        half = out.shape[-1] // 2
-        low, high = pl.ds(0, half), pl.ds(half, half)
+        a, first_col, cols = chunks[m]
+        out = outs[a]
+        half = cols // 2
+        every = pl.ds(first_col, cols)
+        low, high = pl.ds(first_col, half), pl.ds(first_col + half, half)
         if stage == 0:
             for hop in hops:
                 push(
                     m,
                     0,
                     hop,
-                    ins[m].at[c, y, x],
-                    out.at[shard, c, y, x],
+                    ins[a].at[c, y, x, :, every],
+                    out.at[shard, c, y, x, :, every],
                     (rep, lax.rem(shard + hop, count)),
                 )
-            own = pltpu.make_async_copy(ins[m], out.at[shard], local.at[m])
-            own.start()
-            owns.append(own)
+            if first_col == 0:
+                own = pltpu.make_async_copy(ins[a], out.at[shard], local.at[a])
+                own.start()
+                owns.append(own)
         elif stage == 1:
             for hop in hops:
                 started[m, 0, hop].wait_recv()
@@ -152,13 +171,14 @@
                 s = owner(hop)
                 started[m, 3, hop].wait_recv()
                 started[m, 4, hop].wait_recv()
-                push(m, 5, hop, out.at[s, c], out.at[s, c], (core_peer, shard))
+                done = out.at[s, c, :, :, :, every]
+                push(m, 5, hop, done, done, (core_peer, shard))
         else:
             for hop in hops:
                 started[m, 5, hop].wait_recv()
 
-    for time in range(number + 4):
-        for m in range(number):
+    for time in range(len(chunks) + 4):
+        for m in range(len(chunks)):
             if 0 <= time - m <= 4:
                 step(m, time - m)
     for copy in started.values():
@@ -169,15 +189,16 @@
 
 def gather_all(count, arrays):
     number = len(arrays)
+    chunks = cut([(count * a.shape[0], a.shape[1]) for a in arrays])
     split = [a.reshape(2, 2, 2, a.shape[0] // GROUP, a.shape[1]) for a in arrays]
     outs = pl.pallas_call(
-        functools.partial(gather_kernel, count, number),
+        functools.partial(gather_kernel, count, number, chunks),
         out_shape=[jax.ShapeDtypeStruct((count,) + a.shape, a.dtype) for a in split],
         in_specs=[pl.BlockSpec(memory_space=pl.ANY)] * number,
         out_specs=[pl.BlockSpec(memory_space=pl.ANY)] * number,
         scratch_shapes=[
-            pltpu.SemaphoreType.DMA((number, 6, count - 1)),
-            pltpu.SemaphoreType.DMA((number, 6, count - 1)),
+            pltpu.SemaphoreType.DMA((len(chunks), 6, count - 1)),
+            pltpu.SemaphoreType.DMA((len(chunks), 6, count - 1)),
             pltpu.SemaphoreType.DMA((number,)),
         ],
         compiler_params=pltpu.CompilerParams(
@@ -204,11 +225,11 @@
     lax.fori_loop(0, lead * (rows // chunk), body, 0)
 
 
-def reduce_kernel(count, number, *refs):
+def reduce_kernel(count, number, chunks, *refs):
     ins, outs = refs[:number], refs[number : 2 * number]
     scratch = refs[2 * number :]
-    per = [scratch[7 * m : 7 * m + 7] for m in range(number)]
-    send, recv, local = scratch[7 * number :]
+    per = [scratch[7 * m : 7 * m + 7] for m in range(len(chunks))]
+    send, recv, local = scratch[7 * len(chunks) :]
     rep, shard, (c, y, x), core_peer, x_peer, y_peer = peers()
     greet(count)
     started = {}
@@ -220,13 +241,16 @@
 
     def step(m, stage):
         acc, r1, r2a, r2b, r3a, r3b, r4 = per[m]
-        out = outs[m]
-        rows, cols = acc.shape[-2:]
+        a, first_col, cols = chunks[m]
+        out = outs[a]
+        rows = acc.shape[-2]
         half = cols // 2
         low, high = pl.ds(0, half), pl.ds(half, half)
+        every = pl.ds(first_col, cols)
+        out_low, out_high = pl.ds(first_col, half), pl.ds(first_col + half, half)
         if stage == 0:
-            push(m, 0, ins[m].at[:, 1 - c], r1, (core_peer, shard))
-            own = pltpu.make_async_copy(ins[m].at[:, c], acc, local.at[m, 0])
+            push(m, 0, ins[a].at[:, 1 - c, :, :, :, every], r1, (core_peer, shard))
+            own = pltpu.make_async_copy(ins[a].at[:, c, :, :, :, every], acc, local.at[m, 0])
             own.start()
             started[m, "own"] = own
         elif stage == 1:
@@ -282,35 +306,38 @@
                 return carry
 
             lax.fori_loop(0, rows // 16, total, 0)
-            own = pltpu.make_async_copy(acc.at[shard, y, x], out.at[c, y, x], local.at[m, 1])
+            own = pltpu.make_async_copy(
+                acc.at[shard, y, x], out.at[c, y, x, :, every], local.at[m, 1]
+            )
             own.start()
             started[m, "res"] = own
             k = 4 + count
             push(
-                m, k, acc.at[shard, y, x, :, low], out.at[c, y, x, :, low], (x_peer, shard)
+                m, k, acc.at[shard, y, x, :, low], out.at[c, y, x, :, out_low], (x_peer, shard)
             )
             push(
-                m, k + 1, acc.at[shard, y, x, :, high], out.at[c, y, x, :, high], (y_peer, shard)
+                m, k + 1, acc.at[shard, y, x, :, high], out.at[c, y, x, :, out_high], (y_peer, shard)
             )
         elif stage == 5:
             k = 4 + count
             started[m, "res"].wait()
             started[m, k].wait_recv()
-            first = out.at[c, y, :, :, low]
+            first = out.at[c, y, :, :, out_low]
             push(m, k + 2, first, first, (y_peer, shard))
             started[m, k + 1].wait_recv()
-            second = out.at[c, :, x, :, high]
+            second = out.at[c, :, x, :, out_high]
             push(m, k + 3, second, second, (x_peer, shard))
         elif stage == 6:
             k = 4 + count
             started[m, k + 2].wait_recv()
             started[m, k + 3].wait_recv()
-            push(m, k + 4, out.at[c], out.at[c], (core_peer, shard))
+            done = out.at[c, :, :, :, every]
+            push(m, k + 4, done, done, (core_peer, shard))
         else:
             started[m, 8 + count].wait_recv()
 
-    for time in range(number + 7):
-        for m in range(number):
+    for time in range(len(chunks) + 7):
+        for m in range(len(chunks)):
             if 0 <= time - m <= 7:
                 step(m, time - m)
     for (_, k), copy in started.items():
@@ -320,11 +347,14 @@
 
 def reduce_all(count, arrays):
     number = len(arrays)
-    split, scratch = [], []
-    for a in arrays:
-        rows, cols = a.shape[0] // (count * GROUP), a.shape[1]
+    chunks = cut([a.shape for a in arrays])
+    split = [
+        a.reshape(count, 2, 2, 2, a.shape[0] // (count * GROUP), a.shape[1]) for a in arrays
+    ]
+    scratch = []
+    for a, _, cols in chunks:
+        rows = split[a].shape[-2]
         half = cols // 2
-        split.append(a.reshape(count, 2, 2, 2, rows, cols))
         for shape in (
             (count, 2, 2, rows, cols),
             (count, 2, 2, rows, cols),
@@ -336,15 +366,15 @@
         ):
             scratch.append(pltpu.VMEM(shape, jnp.bfloat16))
     outs = pl.pallas_call(
-        functools.partial(reduce_kernel, count, number),
+        functools.partial(reduce_kernel, count, number, chunks),
         out_shape=[jax.ShapeDtypeStruct(a.shape[1:], a.dtype) for a in split],
         in_specs=[pl.BlockSpec(memory_space=pl.ANY)] * number,
         out_specs=[pl.BlockSpec(memory_space=pl.ANY)] * number,
         scratch_shapes=scratch
         + [
-            pltpu.SemaphoreType.DMA((number, 9 + count)),
-            pltpu.SemaphoreType.DMA((number, 9 + count)),
-            pltpu.SemaphoreType.DMA((number, 2)),
+            pltpu.SemaphoreType.DMA((len(chunks), 9 + count)),
+            pltpu.SemaphoreType.DMA((len(chunks), 9 + count)),
+            pltpu.SemaphoreType.DMA((len(chunks), 2)),
         ],
         compiler_params=pltpu.CompilerParams(
             collective_id=1, has_side_effects=True, vmem_limit_bytes=48 * MIB
@@ -589,7 +619,7 @@
         up_shift,
     ) = unpack(small_full, count, sizes)
     rows, width = tokens.shape
-    inputs = tokens.astype(jnp.float32)
+    inputs = by_rows(tokens.astype(jnp.float32))
     normed_one, scale_one = normalize(inputs)
     first = (normed_one * first_gain.astype(jnp.float32) + first_shift.astype(jnp.float32)).astype(
         jnp.bfloat16
@@ -597,6 +627,7 @@
     joined = jnp.concatenate([query_bias, jnp.zeros_like(query_bias), value_bias]).astype(
         jnp.float32
     )
+    first = by_rows(first)
     qkv = (jnp.dot(first, qkv_matrix, preferred_element_type=jnp.float32) + joined).astype(
         jnp.bfloat16
     )
@@ -606,10 +637,12 @@
         + jnp.dot(mixed, out_matrix, preferred_element_type=jnp.float32)
         + out_shift.astype(jnp.float32)
     )
+    middle = by_rows(middle)
     normed_two, scale_two = normalize(middle)
     second = (
         normed_two * second_gain.astype(jnp.float32) + second_shift.astype(jnp.float32)
     ).astype(jnp.bfloat16)
+    second = by_rows(second)
     upper = jnp.dot(second, up_matrix, preferred_element_type=jnp.float32) + up_shift.astype(
         jnp.float32
     )
@@ -629,12 +662,13 @@
     grad_upper = (grad_active * gelu_slope).astype(jnp.bfloat16)
     up_shift_grad = column_sum(grad_upper)
     up_grad = left_dot(second, grad_upper)
-    grad_second = right_dot(grad_upper, up_matrix)
+    grad_second = by_rows(right_dot(grad_upper, up_matrix))
     second_gain_grad = jnp.sum(grad_second * normed_two, axis=0)
     second_shift_grad = jnp.sum(grad_second, axis=0)
     grad_middle = cotangent.astype(jnp.float32) + norm_back(
         grad_second, normed_two, scale_two, second_gain.astype(jnp.float32)
     )
+    grad_middle = by_rows(grad_middle)
     grad_branch = grad_middle.astype(jnp.bfloat16)
     out_shift_grad = column_sum(grad_branch)
     out_grad = left_dot(mixed, grad_branch)
@@ -643,7 +677,7 @@
     query_bias_grad = column_sum(grad_qkv[:, :width])
     value_bias_grad = column_sum(grad_qkv[:, 2 * width :])
     qkv_grad = left_dot(first, grad_qkv)
-    grad_first = right_dot(grad_qkv, qkv_matrix)
+    grad_first = by_rows(right_dot(grad_qkv, qkv_matrix))
     first_gain_grad = jnp.sum(grad_first * normed_one, axis=0)
     first_shift_grad = jnp.sum(grad_first, axis=0)
     token_grad = (

time: 598 us -> 559 us (0.935)
  local copies, waits for them, and re-layouts: 54.8 us -> 23.7 us
  Pallas kernels: 358 us -> 351 us
    unnamed x106 -> x124, local copies, waits for them, and re-layouts: 41.3 us -> 22 us
    dot_general x2 -> x0, local copies, waits for them, and re-layouts: 11 us -> none  [right_dot(): lax.dot_general(left, right, (((1,), (1,)), ((), ())), preferred_element_...]
    reduce_sum x2 -> x0, other arithmetic: 8.01 us -> none  [the longest x1 4.29 us: shards(): second_gain_grad = jnp.sum(grad_second * normed_two, axis=0)]
    pallas_call x2, Pallas kernels: 275 us -> 268 us  [the longest x1 167 us: reduce_all(): pl.pallas_call(functools.partial(reduce_kernel, count, number, chunks), o...]
where the time goes in v2:
time: 559 us; the launch traced here: 550 us
  Pallas kernels  351 us (63%)
  matrix products  143 us (26%)
  other arithmetic  30.4 us (5%)
  local copies, waits for them, and re-layouts  23.7 us (4%)
    pallas_call x1, Pallas kernels, reduce_all(): pl.pallas_call(functools.partial(reduce_kernel, count, number, chunks), o...  167 us
    pallas_call x1, Pallas kernels, gather_all(): pl.pallas_call(functools.partial(gather_kernel, count, number, chunks), o...  101 us
    dot_general x4, matrix products, right_dot(): lax.dot_general(left, right, (((1,), (1,)), ((), ())), preferred_element_...  55.1 us
    pallas_call x1, Pallas kernels, attend_back(): pl.pallas_call(functools.partial(attend_back_kernel, HEADS), grid=(pairs,...  46.9 us
    dot_general x4, matrix products, left_dot(): lax.dot_general(left, right, (((0,), (0,)), ((), ())), preferred_element_...  44.1 us
    pallas_call x1, Pallas kernels, attend(): pl.pallas_call(functools.partial(attend_kernel, HEADS), grid=(pairs,), in...  35.8 us
    unnamed x124, local copies, waits for them, and re-layouts  22 us
    dot_general x1, matrix products, shards(): jnp.dot(active, down_matrix, preferred_element_type=jnp.float32)  16 us

profile of v2, /device:TPU:0, one launch (start us, length us, event | category | flops | bytes accessed | tf_op | source)
XLA Modules:
  0.0 549.7 jit_solution(17761158353904406044)
XLA Ops:
  0.8 2.1 convert_reduce_fusion
  2.9 2.3 fusion.21
  7.3 1.6 copy-done.2
  8.9 1.4 copy-done.6
  10.3 101.0 %gather_parameters.1 = (bf16[4,2,2,2,16,256]{5,4,3,2,1,0:T(8,128)(2,1)S(1)}, bf16[4,2,2,2,32,3072]{5,4,3,2,1,0:T(8,128)(2,1)S(1)}, bf16[4,2,2,2,32,1024]{5,4,3,2...) custom-call(bf16[2,2,2,16,256]{4,3,2,1,0:T(8,128)(2,1)S(1)} %reshape_reshape.9.refs, ...), custom_call_target="tpu_custom_call" | custom-call | tf_op jit(solution)/shard_map/gather_parameters/pallas_call | solution.py:194
  111.3 3.2 copy-done.12
  114.9 2.3 copy-done.13
  117.2 10.4 %add_convert_fusion.q_ref.k_ref.v_ref = bf16[1024,3072]{1,0:T(8,128)(2,1)S(1)} fusion(f32[3072]{0:T(1024)S(1)} %maximum_convert_fusion, bf16[1024,3072]{1,0:T(8,128)(2,1)S(1)} %bitcast.102, bf16[1024,1024]{1,0:T(8,128)(2,1)} %param.16, f32[1024]{0:T(1024)S(1)} %bitcast.126, f32[1024]{0:T(1024)S(1)} %bitcast.113, f32[1024]{0:T(1024)S(1)} %add_rsqrt_fusion.1, ...), kind=kOutput, calls=%fused_computation.10 | convolution fusion | flops 6455033856 | bytes 14708736 | tf_op jit(solution)/shard_map/dot_general | solution.py:631
  127.7 35.8 %attend.1 = (bf16[1024,1024]{1,0:T(8,128)(2,1)S(1)}, f32[8,2,1024]{2,1,0:T(2,128)S(1)}) custom-call(s32[1,1024]{1,0:T(1,128)S(1)} %copy-done.9, s32[1024,1]{1,0:T(8,128)S(1)} %copy.31.seg_col, bf16[1024,3072]{1,0:T(8,128)(2,1)S(1)} %add_convert_fusion.q_ref.k_ref.v_ref, bf16[1024,3072]{1,0:T(8,128)(2,1)S(1)} %add_convert_fusion.q_ref.k_ref.v_ref, ...), custom_call_target="tpu_custom_call" | custom-call | tf_op jit(solution)/shard_map/attend/pallas_call | solution.py:506
  163.5 2.5 fusion.31
  166.0 2.0 copy-done.22
  168.6 14.5 %fusion.27 = f32[1024,4096]{1,0:T(8,128)} fusion(bf16[1024,4096]{1,0:T(8,128)(2,1)S(1)} %bitcast.96, f32[1024,1024]{1,0:T(8,128)} %copy-done.22, f32[1024]{0:T(1024)S(1)} %bitcast.128, f32[1024]{0:T(1024)S(1)} %bitcast.120, f32[1024]{0:T(1024)S(1)} %add_rsqrt_fusion, f32[1024]{0:T(1024)S(1)} %broadcast_multiply_fusion.4), kind=kOutput, calls=%fused_computation.83 | convolution fusion | flops 8595177472 | bytes 29376512 | tf_op jit(solution)/shard_map/dot_general | solution.py:646
  183.1 16.0 %add_convert_fusion.1 = bf16[1024,1024]{1,0:T(8,128)(2,1)} fusion(f32[1024,1024]{1,0:T(8,128)} %copy-done.22, f32[1024]{0:T(1024)S(1)} %bitcast.131, bf16[4096,1024]{1,0:T(8,128)(2,1)S(1)} %bitcast.101, f32[1024,4096]{1,0:T(8,128)} %fusion.27, f32[4096]{0:T(1024)S(1)} %bitcast.117), kind=kOutput, calls=%fused_computation.36 | convolution fusion | flops 8635023360 | bytes 31477760 | tf_op jit(solution)/shard_map/dot_general | solution.py:653
  199.2 25.2 %fusion.32 = (bf16[4096]{0:T(1024)(128)(2,1)S(1)}, bf16[1024,4096]{1,0:T(8,128)(2,1)}) fusion(f32[1024,4096]{1,0:T(8,128)} %fusion.27, f32[4096]{0:T(1024)S(1)} %bitcast.118, bf16[4096,1024]{1,0:T(8,128)(2,1)} %bitcast.98, bf16[1024,1024]{1,0:T(8,128)(2,1)S(1)} %copy-done.26), kind=kOutput, calls=%fused_computation.88 | convolution fusion | flops 8678010880 | bytes 35676160 | tf_op jit(solution)/shard_map/dot_general | solution.py:41
  224.4 18.6 %convolution_convert_fusion.1 = bf16[4096,1024]{1,0:T(8,128)(2,1)} fusion(bf16[1024,1024]{1,0:T(8,128)(2,1)S(1)} %copy-done.26, f32[1024,4096]{1,0:T(8,128)} %fusion.27, f32[4096]{0:T(1024)S(1)} %bitcast.119), kind=kOutput, calls=%fused_computation.12 | convolution fusion | flops 8636071936 | bytes 27279360 | tf_op jit(solution)/shard_map/dot_general | solution.py:35
  243.0 14.2 %multiply_reduce_fusion = (bf16[1024]{0:T(1024)(128)(2,1)S(1)}, f32[1024]{0:T(1024)S(1)}, f32[1024]{0:T(1024)S(1)}, bf16[1024]{0:T(1024)(128)(2,1)S(1)}, f32[1024,1024]{1,0:T(8,128)}) fusion(f32[1024,1024]{1,0:T(8,128)S(1)} %copy-done.23, f32[1024]{0:T(1024)S(1)} %add_rsqrt_fusion, f32[1024]{0:T(1024)S(1)} %broadcast_multiply_fusion.4, ...), kind=kOutput, calls=%fused_computation.33 | convolution fusion | flops 8599367680 | bytes 25190400 | tf_op jit(solution)/shard_map/dot_general | solution.py:41
  257.3 4.6 convert_reduce_fusion.1
  261.9 2.5 copy-done.45
  264.4 12.3 %convolution_convert_fusion = bf16[1024,4096]{1,0:T(8,128)(2,1)} fusion(bf16[1024,4096]{1,0:T(8,128)(2,1)S(1)} %copy-done.45, f32[1024,1024]{1,0:T(8,128)S(1)} %copy-done.24, f32[1024]{0:T(1024)S(1)} %bitcast.129, f32[1024]{0:T(1024)S(1)} %bitcast.123, f32[1024]{0:T(1024)S(1)} %add_rsqrt_fusion, f32[1024]{0:T(1024)S(1)} %broadcast_multiply_fusion.4), kind=kOutput, calls=%fused_computation.11 | convolution fusion | flops 8599371776 | bytes 20987904 | tf_op jit(solution)/shard_map/dot_general | solution.py:35
  276.8 3.7 convolution_convert_fusion.3
  280.5 2.4 convolution_convert_fusion.4.gm_ref
  282.9 46.9 %attend_back.1 = (bf16[1024,1024]{1,0:T(8,128)(2,1)S(1)}, bf16[1024,1024]{1,0:T(8,128)(2,1)S(1)}, bf16[1024,1024]{1,0:T(8,128)(2,1)S(1)}) custom-call(s32[1,1024]{1,0:T(1,128)S(1)} %copy-done.9, s32[1024,1]{1,0:T(8,128)S(1)} %copy.31.seg_col, bf16[1024,3072]{1,0:T(8,128)(2,1)} %copy-done, bf16[1024,3072]{1,0:T(8,128)(2,1)} %copy-done, ...), custom_call_target="tpu_custom_call" | custom-call | tf_op jit(solution)/shard_map/attend_back/pallas_call | solution.py:534
  332.4 3.6 fusion.29
  336.1 1.5 constant_dynamic-update-slice_fusion.1
  338.4 2.1 fusion.28
  340.4 13.2 %fusion.20 = (bf16[1024]{0:T(1024)(128)(2,1)S(1)}, f32[1024]{0:T(1024)S(1)}, f32[1024]{0:T(1024)S(1)}, bf16[1024]{0:T(1024)(128)(2,1)S(1)}, f32[1024,1024]{1,0:T(8,128)}) fusion(bf16[1024,1024]{1,0:T(8,128)(2,1)S(1)} %copy-done.19, f32[1024]{0:T(1024)S(1)} %copy-done.31, f32[1024]{0:T(1024)S(1)} %copy-done.29, f32[1024]{0:T(1024)S(1)} %bitcast.114, ...), kind=kOutput, calls=%fused_computation.30 | convolution fusion | flops 6452932608 | bytes 18898944 | tf_op jit(solution)/shard_map/dot_general | solution.py:41
  353.7 5.4 fusion.19
  359.7 9.5 %convolution_convert_fusion.2 = bf16[1024,3072]{1,0:T(8,128)(2,1)} fusion(bf16[1024,3072]{1,0:T(8,128)(2,1)S(1)} %copy-done.27, bf16[1024,1024]{1,0:T(8,128)(2,1)S(1)} %copy-done.20, f32[1024]{0:T(1024)S(1)} %bitcast.127, f32[1024]{0:T(1024)S(1)} %bitcast.116, f32[1024]{0:T(1024)S(1)} %copy-done.31, f32[1024]{0:T(1024)S(1)} %copy-done.29), kind=kOutput, calls=%fused_computation.16 | convolution fusion | flops 6451888128 | bytes 14696448 | tf_op jit(solution)/shard_map/dot_general | solution.py:35
  369.5 167.5 %reduce_gradients.1 = (bf16[2,2,2,128,1024]{4,3,2,1,0:T(8,128)(2,1)S(1)}, bf16[2,2,2,32,4096]{4,3,2,1,0:T(8,128)(2,1)}, bf16[2,2,2,32,1024]{4,3,2,1,0:T(8,128)(2...) custom-call(bf16[4,2,2,2,128,1024]{5,4,3,2,1,0:T(8,128)(2,1)} %bitcast.106, ...), custom_call_target="tpu_custom_call" | custom-call | tf_op jit(solution)/shard_map/reduce_gradients/pallas_call | solution.py:368
  540.5 3.4 bitcast_convert_fusion.2
  544.0 2.6 bitcast_convert_fusion.1
  546.6 2.6 bitcast_convert_fusion
  (150 shorter events, 11.0 us)
Async XLA Ops:
  0.7 6.4 %copy-start.9 = (s32[1,1024]{1,0:T(1,128)S(1)}, s32[1,1024]{1,0:T(1,128)}, u32[]{:S(2)}) copy-start(s32[1,1024]{1,0:T(1,128)} %seg_row.3) | copy-start | bytes 12292
  0.7 6.1 %copy-start.44 = (bf16[256]{0:T(256)(128)(2,1)S(1)}, bf16[256]{0:T(256)(128)(2,1)}, u32[]{:S(2)}) copy-start(bf16[256]{0:T(256)(128)(2,1)} %param.30) | copy-start | bytes 1540
  0.7 6.3 %copy-start.36 = (bf16[1024]{0:T(1024)(128)(2,1)S(1)}, bf16[1024]{0:T(1024)(128)(2,1)}, u32[]{:S(2)}) copy-start(bf16[1024]{0:T(1024)(128)(2,1)} %param.28) | copy-start | bytes 6148
  0.7 6.6 %copy-start.1 = (bf16[256,4096]{1,0:T(8,128)(2,1)S(1)}, bf16[256,4096]{1,0:T(8,128)(2,1)}, u32[]{:S(2)}) copy-start(bf16[256,4096]{1,0:T(8,128)(2,1)} %param.27) | copy-start | bytes 6291460
  0.7 5.9 %copy-start.43 = (bf16[256]{0:T(256)(128)(2,1)S(1)}, bf16[256]{0:T(256)(128)(2,1)}, u32[]{:S(2)}) copy-start(bf16[256]{0:T(256)(128)(2,1)} %param.26) | copy-start | bytes 1540
  0.7 5.6 %copy-start.42 = (bf16[256]{0:T(256)(128)(2,1)S(1)}, bf16[256]{0:T(256)(128)(2,1)}, u32[]{:S(2)}) copy-start(bf16[256]{0:T(256)(128)(2,1)} %param.25) | copy-start | bytes 1540
  0.7 5.4 copy-start.41
  0.7 6.6 %copy-start.8 = (bf16[256,1024]{1,0:T(8,128)(2,1)S(1)}, bf16[256,1024]{1,0:T(8,128)(2,1)}, u32[]{:S(2)}) copy-start(bf16[256,1024]{1,0:T(8,128)(2,1)} %param.23) | copy-start | bytes 1572868
  0.7 5.2 copy-start.40
  0.7 4.9 copy-start.39
  0.8 4.7 copy-start.38
  2.9 112.1 %copy-start.28 = (f32[1024]{0:T(1024)}, f32[1024]{0:T(1024)S(1)}, u32[]{:S(2)}) copy-start(f32[1024]{0:T(1024)S(1)} %broadcast_multiply_fusion.5) | copy-start | bytes 12292
  5.2 122.4 %copy-start.30 = (f32[1024]{0:T(1024)}, f32[1024]{0:T(1024)S(1)}, u32[]{:S(2)}) copy-start(f32[1024]{0:T(1024)S(1)} %add_rsqrt_fusion.1) | copy-start | bytes 12292
  114.5 48.9 %copy-start.14 = (bf16[4,2,2,2,32,1024]{5,4,3,2,1,0:T(8,128)(2,1)}, bf16[4,2,2,2,32,1024]{5,4,3,2,1,0:T(8,128)(2,1)S(1)}, u32[]{:S(2)}) copy-start(bf16[4,2,2,2,32,1024]{5,4,3,2,1,0:T(8,128)(2,1)S(1)} %get-tuple-element.33) | copy-start | bytes 6291460
  114.5 54.1 %copy-start.10 = (bf16[4,2,2,2,32,4096]{5,4,3,2,1,0:T(8,128)(2,1)}, bf16[4,2,2,2,32,4096]{5,4,3,2,1,0:T(8,128)(2,1)S(1)}, u32[]{:S(2)}) copy-start(bf16[4,2,2,2,32,4096]{5,4,3,2,1,0:T(8,128)(2,1)S(1)} %get-tuple-element.34) | copy-start | bytes 25165828
  114.9 12.8 %copy-start.34 = (f32[1,2,4,128]{3,1,2,0:T(2,128)}, f32[1,2,4,128]{3,1,2,0:T(2,128)S(1)}, u32[]{:S(2)}) copy-start(f32[1,2,4,128]{3,1,2,0:T(2,128)S(1)} %copy.35) | copy-start | bytes 12292
  114.9 12.7 %copy-start.32 = (f32[1,2,4,128]{3,1,2,0:T(2,128)}, f32[1,2,4,128]{3,1,2,0:T(2,128)S(1)}, u32[]{:S(2)}) copy-start(f32[1,2,4,128]{3,1,2,0:T(2,128)S(1)} %copy.34) | copy-start | bytes 12292
  127.6 35.8 %copy-start = (bf16[1024,3072]{1,0:T(8,128)(2,1)}, bf16[1024,3072]{1,0:T(8,128)(2,1)S(1)}, u32[]{:S(2)}) copy-start(bf16[1024,3072]{1,0:T(8,128)(2,1)S(1)} %add_convert_fusion.q_ref.k_ref.v_ref) | copy-start | bytes 18874372
  127.6 35.8 %copy-start.18 = (bf16[1024,1024]{1,0:T(8,128)(2,1)S(1)}, bf16[1024,1024]{1,0:T(8,128)(2,1)}, u32[]{:S(2)}) copy-start(bf16[1024,1024]{1,0:T(8,128)(2,1)} %param.16) | copy-start | bytes 6291460
  168.0 15.1 %slice-start = ((s8[8388608]{0:T(1024)(128)(4,1)}), s8[4194304]{0:T(1024)(128)(4,1)S(1)}, s32[]{:S(2)}) async-start(s8[8388608]{0:T(1024)(128)(4,1)} %bitcast.99), calls=%async_computation | async-start | bytes 8388608
  168.6 14.5 %slice-start.1 = ((s8[8388608]{0:T(1024)(128)(4,1)}), s8[4194304]{0:T(1024)(128)(4,1)S(1)}, s32[]{:S(2)}) async-start(s8[8388608]{0:T(1024)(128)(4,1)} %bitcast.99), calls=%async_computation.1 | async-start | bytes 8388608
  183.1 16.1 %copy-start.26 = (bf16[1024,1024]{1,0:T(8,128)(2,1)S(1)}, bf16[1024,1024]{1,0:T(8,128)(2,1)}, u32[]{:S(2)}) copy-start(bf16[1024,1024]{1,0:T(8,128)(2,1)} %param.31) | copy-start | bytes 6291460
  224.4 18.6 %copy-start.11 = (bf16[4,2,2,2,32,4096]{5,4,3,2,1,0:T(8,128)(2,1)S(1)}, bf16[4,2,2,2,32,4096]{5,4,3,2,1,0:T(8,128)(2,1)}, u32[]{:S(2)}) copy-start(bf16[4,2,2,2,32,4096]{5,4,3,2,1,0:T(8,128)(2,1)} %copy-done.10) | copy-start | bytes 25165828
  224.4 18.6 %copy-start.23 = (f32[1024,1024]{1,0:T(8,128)S(1)}, f32[1024,1024]{1,0:T(8,128)}, u32[]{:S(2)}) copy-start(f32[1024,1024]{1,0:T(8,128)} %copy-done.22) | copy-start | bytes 12582916
  257.2 4.7 copy-start.24
  257.3 7.1 %copy-start.45 = (bf16[1024,4096]{1,0:T(8,128)(2,1)S(1)}, bf16[1024,4096]{1,0:T(8,128)(2,1)}, u32[]{:S(2)}) copy-start(bf16[1024,4096]{1,0:T(8,128)(2,1)} %get-tuple-element.81) | copy-start | bytes 25165828
  264.4 16.1 %copy-start.21 = (f32[1024,1024]{1,0:T(8,128)}, f32[1024,1024]{1,0:T(8,128)S(1)}, u32[]{:S(2)}) copy-start(f32[1024,1024]{1,0:T(8,128)S(1)} %get-tuple-element.54) | copy-start | bytes 12582916
  264.4 12.4 %copy-start.17 = (bf16[1024,1024]{1,0:T(8,128)(2,1)S(1)}, bf16[1024,1024]{1,0:T(8,128)(2,1)}, u32[]{:S(2)}) copy-start(bf16[1024,1024]{1,0:T(8,128)(2,1)} %copy-done.16) | copy-start | bytes 6291460
  340.4 13.2 %copy-start.20 = (bf16[1024,1024]{1,0:T(8,128)(2,1)S(1)}, bf16[1024,1024]{1,0:T(8,128)(2,1)}, u32[]{:S(2)}) copy-start(bf16[1024,1024]{1,0:T(8,128)(2,1)} %param.16) | copy-start | bytes 6291460
  353.7 6.0 %copy-start.27 = (bf16[1024,3072]{1,0:T(8,128)(2,1)S(1)}, bf16[1024,3072]{1,0:T(8,128)(2,1)}, u32[]{:S(2)}) copy-start(bf16[1024,3072]{1,0:T(8,128)(2,1)} %get-tuple-element.57) | copy-start | bytes 18874372
  353.7 6.0 %copy-start.35 = (f32[1,2,4,128]{3,1,2,0:T(2,128)S(1)}, f32[1,2,4,128]{3,1,2,0:T(2,128)}, u32[]{:S(2)}) copy-start(f32[1,2,4,128]{3,1,2,0:T(2,128)} %copy-done.34) | copy-start | bytes 12292
  538.2 5.8 %copy-start.25 = (bf16[2,2,2,32,4096]{4,3,2,1,0:T(8,128)(2,1)S(1)}, bf16[2,2,2,32,4096]{4,3,2,1,0:T(8,128)(2,1)}, u32[]{:S(2)}) copy-start(bf16[2,2,2,32,4096]{4,3,2,1,0:T(8,128)(2,1)} %get-tuple-element.43) | copy-start | bytes 6291460
  (16 other events, 45.4 us)
